TPU v7x, 32 devices: a whole 2x2x4 slice. The times are simulated.
32 devices in a mesh: segment: 4 (over y, core), space: 8 (over z, x).
Axes of the slice: x: 2, y: 2, z: 4, core: 2. Of those that a mesh axis runs over, the one named last changes fastest.
Arguments:
- x_in: bfloat16 [2, 16, 16, 256], P(None, 'space'), may hold values from -17 to 17
- out_cotangent: bfloat16 [2, 16, 16, 256], P(None, 'space'), may hold values from -17 to 17, as said below
- timesteps: int32 [2], replicated, may hold values from 0 to 999
- labels: int32 [2], replicated, may hold values from 0 to 999
- time_weight: bfloat16 [128, 512], replicated, may hold values from -0.5 to 0.5
- label_table: bfloat16 [1000, 512], replicated, may hold values from -5 to 5
- conv_weight: bfloat16 [4, 3, 3, 256, 256], P('segment'), may hold values from -0.125 to 0.125
- mod_weight: bfloat16 [4, 512, 512], P('segment'), may hold values from -0.25 to 0.25
- mod_bias: float32 [4, 512], P('segment'), may hold values from -3 to 3
- norm_gain: float32 [4, 256], P('segment'), may hold values from 0.25 to 1.75
Outputs:
- segment_grads: bfloat16 [4, 2, 16, 16, 256], P('segment', None, 'space')
- conv_grad: float32 [4, 2304, 256], P('segment', 'space')
- mod_grad: float32 [4, 512, 512], P('segment')
Inputs may be any that keep to these rules, and one draw needn't show every extreme that they name: `out_cotangent`: cotangent from the layers after the chain.
All inputs are finite; a program needn't handle non-finite values.
Results may differ from a plain program's by a relative error of at most 0.0076.
Values may be sent and summed in bfloat16 or wider, within the bound.
No kernel may reach another device: no remote copies, remote signals or barrier semaphores. Data moves between devices by JAX's collectives and lax.ppermute only.
A program may use at most 64 MiB of HBM per device.

v0:
```python
import functools
import math

import jax
import jax.numpy as jnp
from jax import lax
from jax.experimental import pallas as pl
from jax.experimental.pallas import tpu as pltpu
from jax.sharding import PartitionSpec as P

GROUPS = 32
EPSILON = 1e-05
PAIR = 2
BLOCK = 128
MOD_PARTS = 4
PREPARE_LIMIT = 60 << 20
CHAIN_LIMIT = 48 << 20
VMEM = pl.BlockSpec(memory_space=pltpu.VMEM)
SMEM = pl.BlockSpec(memory_space=pltpu.SMEM)
ANY = pl.BlockSpec(memory_space=pl.ANY)


def sigmoid(values):
    return 1.0 / (1.0 + jnp.exp(-values))


def over_chunks(count, body):
    if count == 1:
        body(0)
    else:

        def step(i, carry):
            body(i)
            return carry

        lax.fori_loop(0, count, step, 0)


def chunk_start(i, size):
    return 0 if isinstance(i, int) else pl.multiple_of(i * size, size)


def fold_rows(values):
    return jnp.sum(values.reshape(values.shape[0] // 8, 8, values.shape[1]), axis=0)


def column(rows):
    return jnp.sum(rows, axis=0, keepdims=True)


def group_sums(rows, width):
    lanes = lax.broadcasted_iota(jnp.int32, rows.shape, 1)
    size = rows.shape[1]
    step = 1
    while step < width:
        ahead = pltpu.roll(rows, size - step, 1)
        behind = pltpu.roll(rows, step, 1)
        rows = rows + jnp.where((lanes & step) == 0, ahead, behind)
        step *= 2
    return rows


def stack_rows(first, second):
    spot = lax.broadcasted_iota(jnp.int32, (8, first.shape[1]), 0)
    return jnp.where(spot == 0, first, jnp.where(spot == 1, second, 0.0))


class Shape:
    def __init__(self, height, cols, channels, space_count):
        self.cols, self.channels = cols, channels
        self.pixels = height * cols
        self.chunk = cols * max(1, min(self.pixels, 256) // cols)
        self.chunks = self.pixels // self.chunk
        self.width = channels // GROUPS
        self.entries = float(self.pixels * self.width)
        self.padded = self.pixels + 2 * cols
        self.own_rows = height // space_count * cols
        self.slab = 9 * channels // space_count
        step = math.gcd(self.slab, channels)
        self.taps = min(9, -(-(channels - step + self.slab) // channels))
        self.pack = self.slab + self.own_rows + 8
        self.limit = (12 << 20) + self.pixels * channels * 40


def statistics(sh, x_ref):
    zero = jnp.zeros((8, sh.channels), jnp.float32)

    def add(i, sums):
        part = x_ref[pl.ds(chunk_start(i, sh.chunk), sh.chunk), :].astype(jnp.float32)
        return (sums[0] + fold_rows(part), sums[1] + fold_rows(part * part))

    if sh.chunks == 1:
        one, two = add(0, (zero, zero))
    else:
        one, two = lax.fori_loop(0, sh.chunks, add, (zero, zero))
    total = group_sums(stack_rows(column(one), column(two)), sh.width) / sh.entries
    mean = total[0:1]
    return (mean, lax.rsqrt(total[1:2] - mean * mean + EPSILON))


def clear_edges(sh, padded_ref):
    zero = jnp.zeros((3, sh.cols, sh.channels), padded_ref.dtype)
    padded_ref[:, 0 : sh.cols, :] = zero
    padded_ref[:, sh.pixels + sh.cols : sh.padded, :] = zero


def spread(sh, padded_ref, start, values):
    place = pl.ds(start + sh.cols, sh.chunk)
    spot = lax.broadcasted_iota(jnp.int32, values.shape, 0) % sh.cols
    padded_ref[0, place, :] = jnp.where(spot == 0, 0.0, pltpu.roll(values, 1, 0)).astype(jnp.bfloat16)
    padded_ref[1, place, :] = values.astype(jnp.bfloat16)
    padded_ref[2, place, :] = jnp.where(
        spot == sh.cols - 1, 0.0, pltpu.roll(values, sh.chunk - 1, 0)
    ).astype(jnp.bfloat16)


def convolve(sh, padded_ref, start, weight_ref, unit, backward):
    size = min(BLOCK, sh.chunk)
    totals = []
    for first in range(0, sh.chunk, size):
        total = None
        for p in range(3):
            for q in range(3):
                row, col = (2 - p, 2 - q) if backward else (p, q)
                block = padded_ref[col, pl.ds(start + first + row * sh.cols, size), :]
                tap = (3 * p + q) * sh.channels
                weight = weight_ref[unit, tap : tap + sh.channels, :]
                part = lax.dot_general(
                    block,
                    weight,
                    (((1,), (1 if backward else 0,)), ((), ())),
                    preferred_element_type=jnp.float32,
                )
                total = part if total is None else total + part
        totals.append(total)
    return totals[0] if len(totals) == 1 else jnp.concatenate(totals, axis=0)


def activation(sh, x_ref, place, stats, params):
    (mean, inv_std), (factor, shift) = stats, params
    pre = (x_ref[place, :].astype(jnp.float32) - mean) * inv_std * factor + shift
    sigma = sigmoid(pre)
    return pre * sigma, sigma * (1.0 + pre * (1.0 - sigma))


def note_unit(sh, x_ref, params, act_ref, slope_ref, turned=False):
    stats = statistics(sh, x_ref)

    def activate(i):
        place = pl.ds(chunk_start(i, sh.chunk), sh.chunk)
        values, slope = activation(sh, x_ref, place, stats, params)
        if turned:
            act_ref[:, place] = values.T.astype(jnp.bfloat16)
        else:
            act_ref[place, :] = values.astype(jnp.bfloat16)
        slope_ref[place, :] = slope

    over_chunks(sh.chunks, activate)
    return stats


def forward_unit(sh, x_ref, out_ref, params, padded_ref, weight_ref, unit, act_ref=None, slope_ref=None):
    stats = statistics(sh, x_ref)

    def activate(i):
        start = chunk_start(i, sh.chunk)
        place = pl.ds(start, sh.chunk)
        values, slope = activation(sh, x_ref, place, stats, params)
        spread(sh, padded_ref, start, values)
        if act_ref is not None:
            act_ref[place, :] = values.astype(jnp.bfloat16)
            slope_ref[place, :] = slope

    def produce(i):
        start = chunk_start(i, sh.chunk)
        inputs = x_ref[pl.ds(start, sh.chunk), :].astype(jnp.float32)
        z = convolve(sh, padded_ref, start, weight_ref, unit, False)
        out_ref[pl.ds(start, sh.chunk), :] = (inputs + z).astype(jnp.bfloat16)

    over_chunks(sh.chunks, activate)
    over_chunks(sh.chunks, produce)
    return stats


def own_place(sh):
    return pl.ds(pl.multiple_of(lax.axis_index("space") * sh.own_rows, sh.own_rows), sh.own_rows)


def place_upstream(sh, up_ref, padded_ref):
    def place(i):
        start = chunk_start(i, sh.chunk)
        spread(sh, padded_ref, start, up_ref[pl.ds(start, sh.chunk), :].astype(jnp.float32))

    over_chunks(sh.chunks, place)


def backward_unit(sh, x_ref, up_ref, grad_ref, params, known, padded_ref, pre_grad_ref, weight_ref, unit, own=False, placed=False):
    slope_ref, (mean, inv_std) = known
    factor, _ = params
    zero = jnp.zeros((8, sh.channels), jnp.float32)

    def differentiate(i, sums):
        start = chunk_start(i, sh.chunk)
        rows = pl.ds(start, sh.chunk)
        normed = (x_ref[rows, :].astype(jnp.float32) - mean) * inv_std
        pre_grad = convolve(sh, padded_ref, start, weight_ref, unit, True) * slope_ref[rows, :]
        pre_grad_ref[rows, :] = pre_grad
        return (sums[0] + fold_rows(pre_grad), sums[1] + fold_rows(pre_grad * normed))

    if not placed:
        place_upstream(sh, up_ref, padded_ref)
    if sh.chunks == 1:
        sums = differentiate(0, (zero, zero))
    else:
        sums = lax.fori_loop(0, sh.chunks, differentiate, (zero, zero))
    sum_grad, sum_cross = column(sums[0]), column(sums[1])
    means = group_sums(stack_rows(factor * sum_grad, factor * sum_cross), sh.width) / sh.entries
    center, tilt = means[0:1], means[1:2]

    def finish(rows):
        normed = (x_ref[rows, :].astype(jnp.float32) - mean) * inv_std
        back = factor * pre_grad_ref[rows, :] - center - normed * tilt
        grad_ref[rows, :] = (up_ref[rows, :].astype(jnp.float32) + inv_std * back).astype(jnp.bfloat16)

    if own:
        finish(own_place(sh))
    else:
        over_chunks(sh.chunks, lambda i: finish(pl.ds(chunk_start(i, sh.chunk), sh.chunk)))
    return stack_rows(sum_grad, sum_cross)


def weight_products(sh, padded_ref, act_ref, slab_ref, grad_ref, sums, unit, keep_ref, send_ref, turned=False):
    core = lax.axis_index("segment") % PAIR
    space = lax.axis_index("space")
    first_row = space * sh.slab
    first_tap = jnp.minimum(first_row // sh.channels, 9 - sh.taps)
    offset = pl.multiple_of(first_row - first_tap * sh.channels, 8)
    for t in range(sh.taps):
        tap = first_tap + t
        row, col = 2 - tap // 3, 2 - tap % 3
        place = pl.ds(t * sh.channels, sh.channels)

        def product(i):
            start = chunk_start(i, sh.chunk)
            block = padded_ref[col, pl.ds(pl.multiple_of(start + row * sh.cols, 16), sh.chunk), :]
            here = pl.ds(start, sh.chunk)
            return lax.dot_general(
                act_ref[:, here] if turned else act_ref[here, :],
                block,
                (((1 if turned else 0,), (0,)), ((), ())),
                preferred_element_type=jnp.float32,
            )

        if sh.chunks == 1:
            slab_ref[place, :] = product(0)
        else:
            slab_ref[place, :] = jnp.zeros((sh.channels, sh.channels), jnp.float32)

            def accumulate(i):
                slab_ref[place, :] += product(i)

            over_chunks(sh.chunks, accumulate)
    mine = slab_ref[pl.ds(offset, sh.slab), :]
    rows = grad_ref[own_place(sh), :]

    def write(ref):
        ref[0 : sh.slab, :] = mine
        ref[sh.slab : sh.slab + sh.own_rows, :] = rows.astype(jnp.float32)
        ref[sh.slab + sh.own_rows : sh.pack, :] = sums

    @pl.when(core == unit)
    def _():
        write(keep_ref)

    @pl.when(core != unit)
    def _():
        write(send_ref)


def place_of():
    index = lax.axis_index("segment")
    return (index // PAIR, index % PAIR)


def unit_params(params_ref, unit):
    return (params_ref[2 * unit : 2 * unit + 1, :], params_ref[2 * unit + 1 : 2 * unit + 2, :])


def sinusoid_of(time, base):
    half = base // 2
    lanes = lax.broadcasted_iota(jnp.int32, (time.shape[0], base), 1)
    power = jnp.where(lanes < half, lanes, lanes - half).astype(jnp.float32)
    angle = time * jnp.exp(-math.log(10000.0) * power / half)
    turns = jnp.floor(angle * (2.0 / math.pi) + 0.5)
    rest = ((angle - turns * 1.5703125) - turns * 4.83751296997e-4) - turns * 7.54978995489e-8
    square = rest * rest
    sine = rest + rest * square * (
        -1.6666654611e-1 + square * (8.3321608736e-3 - square * 1.9515295891e-4)
    )
    cosine = 1.0 - 0.5 * square + square * square * (
        4.166664568298827e-2 + square * (-1.388731625493765e-3 + square * 2.443315711809948e-5)
    )
    quarter = turns.astype(jnp.int32) + jnp.where(lanes < half, 1, 0)
    value = jnp.where(quarter % 2 == 1, cosine, sine)
    return jnp.where((quarter // 2) % 2 == 1, -value, value).astype(jnp.bfloat16)


def start_all(pairs, sems):
    copies = [pltpu.make_async_copy(a, b, sems.at[i]) for i, (a, b) in enumerate(pairs)]
    for copy in copies:
        copy.start()
    return copies


def embed_kernel(times_ref, labels_ref, table_hbm, time_weight_hbm, embedded_ref, table_ref, time_weight_ref, sems):
    pairs = [(time_weight_hbm, time_weight_ref)]
    pairs += [(table_hbm.at[pl.ds(labels_ref[i] // 8, 1)], table_ref.at[pl.ds(i, 1)]) for i in range(PAIR)]
    copies = start_all(pairs, sems)
    spot = lax.broadcasted_iota(jnp.int32, (16, 1), 0)
    time = jnp.where(spot % 2 == 0, times_ref[0], times_ref[1]).astype(jnp.float32)
    sinusoid = sinusoid_of(time, time_weight_ref.shape[0])

    def label_row(image):
        block = table_ref[image].astype(jnp.float32)
        row = lax.broadcasted_iota(jnp.int32, block.shape, 0)
        return column(jnp.where(row == labels_ref[image] % 8, block, 0.0))

    for copy in copies:
        copy.wait()
    timed = jnp.dot(sinusoid, time_weight_ref[...], preferred_element_type=jnp.float32)
    timed = timed + jnp.where(spot % 2 == 0, label_row(0), label_row(1))
    embedded_ref[...] = (timed * sigmoid(timed)).astype(jnp.bfloat16)


def modulate_kernel(embedded_hbm, mod_weight_hbm, bias_hbm, gain_hbm, keep_ref, send_ref, *scratch):
    embedded_ref, mod_weight_ref, bias_ref, gain_ref, sems = scratch
    core = lax.axis_index("segment") % PAIR
    copies = start_all(zip((embedded_hbm, mod_weight_hbm, bias_hbm, gain_hbm), scratch[:4]), sems)
    for copy in copies:
        copy.wait()
    modulation = jnp.dot(embedded_ref[...], mod_weight_ref[...], preferred_element_type=jnp.float32) + bias_ref[...]
    channels = gain_ref.shape[1]
    factor = gain_ref[...] * (1.0 + modulation[:, :channels])
    shift = modulation[:, channels:]
    first = stack_rows(factor[0:1], shift[0:1])
    second = stack_rows(factor[1:2], shift[1:2])
    keep_ref[...] = jnp.where(core == 0, first, second)
    send_ref[...] = jnp.where(core == 0, second, first)


def layout_kernel(own_any, other_any, mod_keep_any, mod_other_any, weights_ref, params_ref, mods_ref, sems):
    core = lax.axis_index("segment") % PAIR
    pairs = [(mod_keep_any, mods_ref.at[core]), (mod_other_any, mods_ref.at[1 - core])]
    pairs += [(own_any, weights_ref.at[core]), (other_any, weights_ref.at[1 - core])]
    copies = start_all(pairs, sems)
    for copy in copies[:PAIR]:
        copy.wait()
    params_ref[0:2, :] = mods_ref[0, 0:2, :]
    params_ref[2:4, :] = mods_ref[1, 0:2, :]
    params_ref[4:8, :] = jnp.zeros((4, params_ref.shape[1]), jnp.float32)
    for copy in copies[PAIR:]:
        copy.wait()


def assemble(sh, blocks_ref, order, image_ref):
    space = lax.axis_index("space")
    for k, bits in enumerate(order):
        start = pl.multiple_of((space ^ bits) * sh.own_rows, sh.own_rows)
        image_ref[pl.ds(start, sh.own_rows), :] = blocks_ref[k]


def forward_kernel(sh, active_stage, orders, *refs):
    if orders:
        near_ref, far_ref, params_ref, weights, x_ref = refs[:5]
        assemble(sh, near_ref, orders[0], x_ref)
        assemble(sh, far_ref, orders[1], x_ref)
        refs = refs[5:]
    else:
        x_ref, params_ref, weights = refs[:3]
        refs = refs[3:]
    middle_ref, out_ref, padded_ref = refs
    stage, _ = place_of()

    @pl.when(stage == active_stage)
    def _():
        clear_edges(sh, padded_ref)
        forward_unit(sh, x_ref, middle_ref, unit_params(params_ref, 0), padded_ref, weights, 0)
        forward_unit(sh, middle_ref, out_ref, unit_params(params_ref, 1), padded_ref, weights, 1)


def note_kernel(sh, active_stage, x_ref, middle_ref, params_ref, *refs):
    act_ref, slope_ref, stats_ref = refs[-3:]
    stage, _ = place_of()

    @pl.when(stage == active_stage)
    def _():
        for unit, source in enumerate((x_ref, middle_ref)):
            stats = note_unit(sh, source, unit_params(params_ref, unit), act_ref.at[unit], slope_ref.at[unit], True)
            stats_ref[unit] = stack_rows(*stats)


def lay_kernel(sh, active_stage, up_ref, padded_ref):
    stage, _ = place_of()

    @pl.when(stage == active_stage)
    def _():
        clear_edges(sh, padded_ref)
        place_upstream(sh, up_ref, padded_ref)


def turn_kernel(sh, active_stage, x_ref, up_ref, laid_ref, params_ref, weights, *refs):
    grad_ref, between_ref, act_ref, sums_ref, padded_ref, pre_grad_ref, middle_ref, slope_ref = refs
    stage, _ = place_of()

    @pl.when(stage == active_stage)
    def _():
        clear_edges(sh, padded_ref)
        params = [unit_params(params_ref, unit) for unit in range(PAIR)]
        acts, slopes = [[ref.at[unit] for unit in range(PAIR)] for ref in (act_ref, slope_ref)]
        first = forward_unit(sh, x_ref, middle_ref, params[0], padded_ref, weights, 0, acts[0], slopes[0])
        second = note_unit(sh, middle_ref, params[1], acts[1], slopes[1])
        work = (pre_grad_ref, weights)
        known = (slopes[1], second)
        sums_ref[1] = backward_unit(
            sh, middle_ref, up_ref, between_ref, params[1], known, laid_ref, *work, 1, placed=True
        )
        known = (slopes[0], first)
        sums_ref[0] = backward_unit(sh, x_ref, between_ref, grad_ref, params[0], known, padded_ref, *work, 0)


def products_kernel(sh, active_stage, laid_ref, between_ref, grad_ref, act_ref, sums_ref, *refs):
    keep_ref, send_ref, padded_ref, slab_ref = refs
    stage, _ = place_of()

    @pl.when(stage == active_stage)
    def _():
        clear_edges(sh, padded_ref)
        place_upstream(sh, between_ref, padded_ref)
        for unit, above, below in ((1, laid_ref, between_ref), (0, padded_ref, grad_ref)):
            outs = (keep_ref, send_ref)
            weight_products(sh, above, act_ref.at[unit], slab_ref, below, sums_ref[unit], unit, *outs)


def backward_kernel(sh, active_stage, *refs):
    x_ref, middle_ref, up_ref, params_ref, weights, act_ref, slope_ref, stats_ref = refs[:8]
    keep_ref, send_ref, grad_ref, padded_ref, pre_grad_ref, slab_ref, between_ref = refs[10:]
    stage, _ = place_of()

    @pl.when(stage == active_stage)
    def _():
        clear_edges(sh, padded_ref)
        for unit, x, above, below in ((1, middle_ref, up_ref, between_ref), (0, x_ref, between_ref, grad_ref)):
            stats = (stats_ref[unit, 0:1, :], stats_ref[unit, 1:2, :])
            known = (slope_ref.at[unit], stats)
            params = unit_params(params_ref, unit)
            own = unit == 0 and active_stage == 0
            sums = backward_unit(sh, x, above, below, params, known, padded_ref, pre_grad_ref, weights, unit, own)
            outs = (keep_ref, send_ref)
            weight_products(sh, padded_ref, act_ref.at[unit], slab_ref, below, sums, unit, *outs, turned=True)


def finish_kernel(sh, keep_ref, other_ref, embedded_ref, gain_ref, grads_hbm, conv_hbm, mod_hbm, *scratch):
    grads_ref, conv_ref, mod_ref, sems = scratch
    core = lax.axis_index("segment") % PAIR
    base = sh.slab + sh.own_rows

    def mod_rows(ref):
        return jnp.concatenate([gain_ref[...] * ref[base + 1 : base + 2, :], ref[base : base + 1, :]], axis=1)

    own, other = mod_rows(keep_ref), mod_rows(other_ref)
    spot = lax.broadcasted_iota(jnp.int32, (16, own.shape[1]), 0)
    values = jnp.where(spot % 2 == core, own, other)
    high = values.astype(jnp.bfloat16).astype(jnp.float32)
    rest = values - high
    middle = rest.astype(jnp.bfloat16).astype(jnp.float32)
    low = rest - middle
    part = spot // 2
    pieces = jnp.where(part == 0, high, jnp.where(part == 1, middle, jnp.where(part == 2, low, 0.0)))
    pieces = pieces.astype(jnp.bfloat16)
    copies = []
    size = mod_ref.shape[0] // MOD_PARTS
    for k in range(MOD_PARTS):
        place = slice(k * size, (k + 1) * size)
        mod_ref[place, :] = lax.dot_general(
            embedded_ref[:, place],
            pieces,
            (((0,), (0,)), ((), ())),
            preferred_element_type=jnp.float32,
        )
        copies.append(pltpu.make_async_copy(mod_ref.at[place], mod_hbm.at[place], sems.at[k]))
        copies[-1].start()
    conv_ref[...] = keep_ref[0 : sh.slab, :] + other_ref[0 : sh.slab, :]
    copies.append(pltpu.make_async_copy(conv_ref, conv_hbm, sems.at[MOD_PARTS]))
    copies[-1].start()
    rows = slice(sh.slab, sh.slab + sh.own_rows)
    grads_ref[pl.ds(core, 1)] = keep_ref[rows, :].astype(jnp.bfloat16)[None]
    grads_ref[pl.ds(1 - core, 1)] = other_ref[rows, :].astype(jnp.bfloat16)[None]
    copies.append(pltpu.make_async_copy(grads_ref, grads_hbm, sems.at[MOD_PARTS + 1]))
    copies[-1].start()
    for copy in copies:
        copy.wait()


def shards(
    x_in,
    out_cotangent,
    timesteps,
    labels,
    time_weight,
    label_table,
    conv_weight,
    mod_weight,
    mod_bias,
    norm_gain,
):
    segments, spaces = lax.axis_size("segment"), lax.axis_size("space")
    stages = segments // PAIR
    stage, core = place_of()
    images, row_count, cols, channels = x_in.shape
    sh = Shape(row_count * spaces, cols, channels, spaces)
    f32, bf16 = jnp.float32, jnp.bfloat16

    def call(body, ins, outs, scratch=(), limit=CHAIN_LIMIT, cost=None, aliases={}):
        return pl.pallas_call(
            body,
            out_shape=outs,
            in_specs=ins,
            out_specs=[VMEM] * len(outs),
            scratch_shapes=list(scratch),
            input_output_aliases=aliases,
            compiler_params=pltpu.CompilerParams(vmem_limit_bytes=limit),
            cost_estimate=cost,
        )

    shape = jax.ShapeDtypeStruct
    swap = [(i, i ^ 1) for i in range(segments)]
    weight = conv_weight.reshape(9 * channels, channels)
    other_weight = lax.ppermute(weight, "segment", swap)
    ends = jnp.where(stage == 0, x_in, out_cotangent)
    near = lax.dynamic_index_in_dim(ends, core, 0, keepdims=False).reshape(1, sh.own_rows, channels)
    table = label_table.reshape(-1, 8, label_table.shape[1])
    width = time_weight.shape[1]
    some = pl.CostEstimate(flops=1 << 20, bytes_accessed=4 << 20, transcendentals=0)
    order, bit = [0], spaces // 2
    waiting = []
    while True:
        far = lax.ppermute(near, "space", [(i, i ^ bit) for i in range(spaces)])
        if not waiting:
            (embedded,) = call(
                embed_kernel,
                [SMEM, SMEM, ANY, ANY],
                [shape((16, width), bf16)],
                [
                    pltpu.VMEM((PAIR, 8, width), bf16),
                    pltpu.VMEM(time_weight.shape, bf16),
                    pltpu.SemaphoreType.DMA((PAIR + 1,)),
                ],
                PREPARE_LIMIT,
                some,
            )(timesteps, labels, table, time_weight)
            waiting = [embedded]
            far, embedded = lax.optimization_barrier((far, embedded))
        elif len(waiting) == 1:
            operands = (embedded, mod_weight[0], mod_bias, norm_gain)
            mod_keep, mod_send = call(
                modulate_kernel,
                [ANY] * 4,
                [shape((8, channels), f32)] * 2,
                [pltpu.VMEM(value.shape, value.dtype) for value in operands] + [pltpu.SemaphoreType.DMA((4,))],
                PREPARE_LIMIT,
                some,
            )(*operands)
            waiting.append(mod_keep)
            far, mod_keep, mod_send = lax.optimization_barrier((far, mod_keep, mod_send))
        far_order = [k ^ bit for k in order]
        if bit == 1:
            break
        near = jnp.concatenate([near, far])
        order, bit = order + far_order, bit // 2
    mod_other = lax.ppermute(mod_send, "segment", swap)
    weights, params = call(
        layout_kernel,
        [ANY] * 4,
        [shape((PAIR, 9 * channels, channels), bf16), shape((8, channels), f32)],
        [pltpu.VMEM((PAIR, 8, channels), f32), pltpu.SemaphoreType.DMA((2 * PAIR,))],
        cost=some,
    )(weight, other_weight, mod_keep, mod_other)

    image_shape = shape((sh.pixels, channels), bf16)
    pack_shape = shape((sh.pack, channels), f32)
    common = [pltpu.VMEM((3, sh.padded, channels), bf16)]

    def hop(value, source, target):
        pairs = [(PAIR * source + k, PAIR * target + k) for k in range(PAIR)]
        return lax.ppermute(value, "segment", pairs + [(b, a) for a, b in pairs])

    image, middle, out = call(
        functools.partial(forward_kernel, sh, 0, (order, far_order)),
        [VMEM] * 4,
        [image_shape] * 3,
        common,
    )(near, far, params, weights)
    entering, middles = [image, hop(out, 0, 1)], [middle]
    for active in range(1, stages - 1):
        middle, out = call(
            functools.partial(forward_kernel, sh, active, None),
            [VMEM] * 3,
            [image_shape, image_shape],
            common,
        )(entering[active], params, weights)
        middles.append(middle)
        entering.append(hop(out, active, active + 1))

    noted = []
    for active in range(stages - 1):
        noted = call(
            functools.partial(note_kernel, sh, active),
            [VMEM] * (3 + len(noted)),
            [
                shape((PAIR, channels, sh.pixels), bf16),
                shape((PAIR, sh.pixels, channels), f32),
                shape((PAIR, 8, channels), f32),
            ],
            cost=some,
            aliases={3 + k: k for k in range(len(noted))},
        )(entering[active], middles[active], params, *noted)

    work = common + [pltpu.VMEM((sh.pixels, channels), f32)]
    slab = [pltpu.VMEM((sh.taps * channels, channels), f32)]
    pair_shape = shape((PAIR, sh.pixels, channels), bf16)
    (laid,) = call(
        functools.partial(lay_kernel, sh, stages - 1),
        [VMEM],
        [shape((3, sh.padded, channels), bf16)],
        cost=some,
    )(image)
    *grad, between, act, sums = call(
        functools.partial(turn_kernel, sh, stages - 1),
        [VMEM] * 5,
        [image_shape, image_shape, pair_shape, shape((PAIR, 8, channels), f32)],
        work + [pltpu.VMEM((sh.pixels, channels), bf16), pltpu.VMEM((PAIR, sh.pixels, channels), f32)],
    )(entering[stages - 1], image, laid, params, weights)
    keep, send = call(
        functools.partial(products_kernel, sh, stages - 1),
        [VMEM] * 5,
        [pack_shape, pack_shape],
        common + slab,
        cost=some,
    )(laid, between, grad[0], act, sums)
    for active in range(stages - 2, -1, -1):
        upstream = hop(grad[0], active + 1, active)
        last = active == 0
        spare = [pltpu.VMEM((sh.pixels, channels), bf16)]
        keep, send, *grad = call(
            functools.partial(backward_kernel, sh, active),
            [VMEM] * 10,
            [pack_shape, pack_shape] + ([] if last else [image_shape]),
            (spare if last else []) + work + slab + spare,
            aliases={8: 0, 9: 1},
        )(entering[active], middles[active], upstream, params, weights, *noted, keep, send)
    other = lax.ppermute(send, "segment", swap)
    finals = [
        ((images, sh.own_rows, channels), bf16),
        ((sh.slab, channels), f32),
        ((width, 2 * channels), f32),
    ]
    grads, conv_grad, mod_grad = pl.pallas_call(
        functools.partial(finish_kernel, sh),
        out_shape=[shape(*final) for final in finals],
        in_specs=[VMEM] * 4,
        out_specs=[ANY] * 3,
        scratch_shapes=[pltpu.VMEM(*final) for final in finals] + [pltpu.SemaphoreType.DMA((MOD_PARTS + 2,))],
        compiler_params=pltpu.CompilerParams(vmem_limit_bytes=CHAIN_LIMIT),
    )(keep, other, embedded, norm_gain)
    return (grads.reshape(1, images, row_count, cols, channels), conv_grad[None], mod_grad[None])


def solution(mesh):
    placed = (
        P(None, "space", None, None),
        P(None, "space", None, None),
        P(),
        P(),
        P(),
        P(),
        P("segment", None, None, None, None),
        P("segment", None, None),
        P("segment", None),
        P("segment", None),
    )
    return jax.shard_map(
        shards,
        mesh=mesh,
        in_specs=placed,
        out_specs=(
            P("segment", None, "space", None, None),
            P("segment", "space", None),
            P("segment", None, None),
        ),
        check_vma=False,
    )
```

profile of v0, /device:TPU:0, one launch (start us, length us, event | category | flops | bytes accessed | tf_op | source)
XLA Modules:
  0.0 35.4 jit_solution(17925259795493365313)
XLA Ops:
  0.6 0.5 %collective-permute-start.3 = (bf16[2304,256]{1,0:T(8,128)(2,1)}, bf16[2304,256]{1,0:T(8,128)(2,1)S(1)}, u32[]{:S(2)}, u32[]{:S(2)}) collective-permute-start(bf16[2304,256]{1,0:T(8,128)(2,1)} %bitcast.7), channel_id=1, source_target_pairs={{0,8},{8,0},{16,24},{24,16},{1,9},{9,1},{17,25},{25,17},{2,10},{10... | collective-permute-start | bytes 3538952 | tf_op jit(solution)/shard_map/ppermute | solution.py:538
  1.2 0.7 %dynamic-slice_select_fusion = bf16[1,2,16,256]{3,2,1,0:T(8,128)(2,1)S(1)} fusion(bf16[2,2,16,256]{3,2,1,0:T(8,128)(2,1)} %param.11, s32[]{:T(128)S(6)} %select_n.27, bf16[2,2,16,256]{3,2,1,0:T(8,128)(2,1)} %param.10, pred[]{:T(512)S(6)} %eq.5), kind=kLoop, calls=%fused_computation.2 | loop fusion | flops 8192 | bytes 49157 | tf_op jit(solution)/shard_map/jit(_where)/select_n | solution.py:539
  1.9 3.7 %collective-permute-start = (bf16[1,32,256]{2,1,0:T(8,128)(2,1)S(1)}, bf16[1,32,256]{2,1,0:T(8,128)(2,1)S(1)}, u32[]{:S(2)}, u32[]{:S(2)}) collective-permute-start(bf16[1,32,256]{2,1,0:T(8,128)(2,1)S(1)} %bitcast.11), channel_id=1, source_target_pairs={{0,4},{1,5},{2,6},{3,7},{4,0},{5,1},{6,2},{7,3},{8,12},{9,13},{10,... | collective-permute-start | bytes 49160 | tf_op jit(solution)/shard_map/ppermute | solution.py:547
  5.6 2.4 %shard_map.121.embedded_hbm.embedded_ref = bf16[16,512]{1,0:T(8,128)(2,1)} custom-call(s32[2]{0:T(128)} %times_ref.1, s32[2]{0:T(128)} %labels_ref.1, bf16[125,8,512]{2,1,0:T(8,128)(2,1)} %bitcast.9, bf16[128,512]{1,0:T(8,128)(2,1)} %time_weight_hbm.1), custom_call_target="tpu_custom_call" | custom-call | flops 1048576 | bytes 4194304 | tf_op jit(solution)/shard_map/pallas_call | solution.py:549
  8.0 0.0 collective-permute-done
  8.0 1.6 %collective-permute-start.1 = (bf16[2,32,256]{2,1,0:T(8,128)(2,1)S(1)}, bf16[2,32,256]{2,1,0:T(8,128)(2,1)S(1)}, u32[]{:S(2)}, u32[]{:S(2)}) collective-permute-start(bf16[2,32,256]{2,1,0:T(8,128)(2,1)S(1)} %pad_maximum_fusion.1), channel_id=1, source_target_pairs={{0,2},{1,3},{2,0},{3,1},{4,6},{5,7},{6,4},{7,5},{8,10},{9,11},{10,... | collective-permute-start | bytes 98312 | tf_op jit(solution)/shard_map/ppermute | solution.py:547
  9.6 1.9 %shard_map.122 = (f32[8,256]{1,0:T(8,128)}, f32[8,256]{1,0:T(8,128)}) custom-call(bf16[16,512]{1,0:T(8,128)(2,1)} %shard_map.121.embedded_hbm.embedded_ref, bf16[512,512]{1,0:T(8,128)(2,1)} %bitcast.10, f32[1,512]{1,0:T(1,128)} %bias_hbm.1, f32[1,256]{1,0:T(1,128)} %gain_ref.1), custom_call_target="tpu_custom_call" | custom-call | flops 1048576 | bytes 4194304 | tf_op jit(solution)/shard_map/pallas_call | solution.py:565
  11.5 0.4 %collective-permute-done.1 = bf16[2,32,256]{2,1,0:T(8,128)(2,1)S(1)} collective-permute-done((bf16[2,32,256]{2,1,0:T(8,128)(2,1)S(1)}, bf16[2,32,256]{2,1,0:T(8,128)(2,1)S(1)}, u32[]{:S(2)}, u32[]{:S(2)}) %collective-permute-start.1) | collective-permute-done | bytes 32800 | tf_op jit(solution)/shard_map/ppermute | solution.py:547
  12.0 1.6 %collective-permute-start.2 = (bf16[4,32,256]{2,1,0:T(8,128)(2,1)S(1)}, bf16[4,32,256]{2,1,0:T(8,128)(2,1)S(1)}, u32[]{:S(2)}, u32[]{:S(2)}) collective-permute-start(bf16[4,32,256]{2,1,0:T(8,128)(2,1)S(1)} %pad_maximum_fusion.refs_0_), channel_id=1, source_target_pairs={{0,1},{1,0},{2,3},{3,2},{4,5},{5,4},{6,7},{7,6},{8,9},{9,8},{10,11... | collective-permute-start | bytes 196616 | tf_op jit(solution)/shard_map/ppermute | solution.py:547
  13.5 0.0 collective-permute-start.4
  13.5 1.4 %collective-permute-done.4.mod_other_any = f32[8,256]{1,0:T(8,128)S(1)} collective-permute-done((f32[8,256]{1,0:T(8,128)}, f32[8,256]{1,0:T(8,128)S(1)}, u32[]{:S(2)}, u32[]{:S(2)}) %collective-permute-start.4) | collective-permute-done | bytes 8224 | tf_op jit(solution)/shard_map/ppermute | solution.py:580
  14.9 0.7 %copy-done.2 = f32[8,256]{1,0:T(8,128)S(1)} copy-done((f32[8,256]{1,0:T(8,128)S(1)}, f32[8,256]{1,0:T(8,128)}, u32[]{:S(2)}) %copy-start.2) | copy-done | bytes 8216
  15.6 0.5 %shard_map.123 = (bf16[2,2304,256]{2,1,0:T(8,128)(2,1)S(1)}, f32[8,256]{1,0:T(8,128)S(1)}) custom-call(bf16[2304,256]{1,0:T(8,128)(2,1)S(1)} %bitcast.8, bf16[2304,256]{1,0:T(8,128)(2,1)S(1)} %collective-permute-done.3.other_any, f32[8,256]{1,0:T(8,128)S(1)} %copy-done.2, f32[8,256]{1,0:T(8,128)S(1)} %collective-permute-done.4.mod_other_any), custom_call_target="tpu_custom_call" | custom-call | flops 1048576 | bytes 4194304 | tf_op jit(solution)/shard_map/pallas_call | solution.py:581
  16.2 0.2 collective-permute-done.2.refs_1_
  16.3 1.6 %shard_map.124 = (bf16[256,256]{1,0:T(8,128)(2,1)S(1)}, bf16[256,256]{1,0:T(8,128)(2,1)S(1)}, bf16[256,256]{1,0:T(8,128)(2,1)S(1)}) custom-call(bf16[4,32,256]{2,1,0:T(8,128)(2,1)S(1)} %pad_maximum_fusion.refs_0_, bf16[4,32,256]{2,1,0:T(8,128)(2,1)S(1)} %collective-permute-done.2.refs_1_, f32[8,256]{1,0:T(8,128)S(1)} %get-tuple-element.36.refs_2_.params_ref.refs_3_, ...), custom_call_target="tpu_custom_call" | custom-call | tf_op jit(solution)/shard_map/pallas_call | solution.py:597
  17.9 0.1 collective-permute-start.5
  18.0 5.4 %collective-permute-done.5.x_ref = bf16[256,256]{1,0:T(8,128)(2,1)S(1)} collective-permute-done((bf16[256,256]{1,0:T(8,128)(2,1)S(1)}, bf16[256,256]{1,0:T(8,128)(2,1)S(1)}, u32[]{:S(2)}, u32[]{:S(2)}) %collective-permute-start.5) | collective-permute-done | bytes 131104 | tf_op jit(solution)/shard_map/ppermute | solution.py:595
  23.4 3.3 %collective-permute-start.6 = (bf16[256,256]{1,0:T(8,128)(2,1)S(1)}, bf16[256,256]{1,0:T(8,128)(2,1)S(1)}, u32[]{:S(2)}, u32[]{:S(2)}) collective-permute-start(bf16[256,256]{1,0:T(8,128)(2,1)S(1)} %get-tuple-element.41.grad_ref), channel_id=1, source_target_pairs={{16,0},{24,8},{0,16},{8,24},{17,1},{25,9},{1,17},{9,25},{18,2},{26... | collective-permute-start | bytes 393224 | tf_op jit(solution)/shard_map/ppermute | solution.py:595
  26.7 0.6 %shard_map.127 = (bf16[2,256,256]{2,1,0:T(8,128)(2,1)S(1)}, f32[2,256,256]{2,1,0:T(8,128)S(1)}, f32[2,8,256]{2,1,0:T(8,128)S(1)}) custom-call(bf16[256,256]{1,0:T(8,128)(2,1)S(1)} %get-tuple-element.38.up_ref.x_ref.refs_0_, bf16[256,256]{1,0:T(8,128)(2,1)S(1)} %get-tuple-element.39.middle_ref.refs_1_, f32[8,256]{1,0:T(8,128)S(1)} %get-tuple-element.36.refs_2_.params_ref.refs_3_), custom_call_target="tpu_custom_call" | custom-call | flops 1048576 | bytes 4194304 | tf_op jit(solution)/shard_map/pallas_call | solution.py:616
  27.4 2.5 %collective-permute-done.6.refs_2_ = bf16[256,256]{1,0:T(8,128)(2,1)S(1)} collective-permute-done((bf16[256,256]{1,0:T(8,128)(2,1)S(1)}, bf16[256,256]{1,0:T(8,128)(2,1)S(1)}, u32[]{:S(2)}, u32[]{:S(2)}) %collective-permute-start.6) | collective-permute-done | bytes 131104 | tf_op jit(solution)/shard_map/ppermute | solution.py:595
  29.9 2.5 %shard_map.129 = (f32[328,256]{1,0:T(8,128)S(1)}, f32[328,256]{1,0:T(8,128)S(1)}) custom-call(bf16[256,256]{1,0:T(8,128)(2,1)S(1)} %get-tuple-element.38.up_ref.x_ref.refs_0_, bf16[256,256]{1,0:T(8,128)(2,1)S(1)} %get-tuple-element.39.middle_ref.refs_1_, ...), custom_call_target="tpu_custom_call", output_to_operand_aliasing={{0}: (8, {}), {1}: (9, {})} | custom-call | tf_op jit(solution)/shard_map/pallas_call | solution.py:654
  32.4 0.1 collective-permute-start.7
  32.5 1.6 %collective-permute-done.7.other_ref = f32[328,256]{1,0:T(8,128)S(1)} collective-permute-done((f32[328,256]{1,0:T(8,128)S(1)}, f32[328,256]{1,0:T(8,128)S(1)}, u32[]{:S(2)}, u32[]{:S(2)}) %collective-permute-start.7) | collective-permute-done | bytes 335904 | tf_op jit(solution)/shard_map/ppermute | solution.py:661
  34.1 1.3 %shard_map.130 = (bf16[2,32,256]{2,1,0:T(8,128)(2,1)}, f32[288,256]{1,0:T(8,128)}, f32[512,512]{1,0:T(8,128)}) custom-call(f32[328,256]{1,0:T(8,128)S(1)} %get-tuple-element.50.keep_ref, f32[328,256]{1,0:T(8,128)S(1)} %collective-permute-done.7.other_ref, bf16[16,512]{1,0:T(8,128)(2,1)S(1)} %copy-done.1, f32[1,256]{1,0:T(1,128)S(1)} %copy-done.3), custom_call_target="tpu_custom_call" | custom-call | tf_op jit(solution)/shard_map/pallas_call | solution.py:667
  (13 shorter events, 0.1 us)
Async XLA Ops:
  0.6 14.3 %copy-start = (bf16[1,3,3,256,256]{4,3,2,1,0:T(8,128)(2,1)S(1)}, bf16[1,3,3,256,256]{4,3,2,1,0:T(8,128)(2,1)}, u32[]{:S(2)}) copy-start(bf16[1,3,3,256,256]{4,3,2,1,0:T(8,128)(2,1)} %param.16) | copy-start | bytes 3538948
  0.6 14.3 %collective-permute-start.3 = (bf16[2304,256]{1,0:T(8,128)(2,1)}, bf16[2304,256]{1,0:T(8,128)(2,1)S(1)}, u32[]{:S(2)}, u32[]{:S(2)}) collective-permute-start(bf16[2304,256]{1,0:T(8,128)(2,1)} %bitcast.7), channel_id=1, source_target_pairs={{0,8},{8,0},{16,24},{24,16},{1,9},{9,1},{17,25},{25,17},{2,10},{10... | collective-permute-start | bytes 3538952 | tf_op jit(solution)/shard_map/ppermute | solution.py:538
  1.9 6.1 %collective-permute-start = (bf16[1,32,256]{2,1,0:T(8,128)(2,1)S(1)}, bf16[1,32,256]{2,1,0:T(8,128)(2,1)S(1)}, u32[]{:S(2)}, u32[]{:S(2)}) collective-permute-start(bf16[1,32,256]{2,1,0:T(8,128)(2,1)S(1)} %bitcast.11), channel_id=1, source_target_pairs={{0,4},{1,5},{2,6},{3,7},{4,0},{5,1},{6,2},{7,3},{8,12},{9,13},{10,... | collective-permute-start | bytes 49160 | tf_op jit(solution)/shard_map/ppermute | solution.py:547
  8.0 4.0 %collective-permute-start.1 = (bf16[2,32,256]{2,1,0:T(8,128)(2,1)S(1)}, bf16[2,32,256]{2,1,0:T(8,128)(2,1)S(1)}, u32[]{:S(2)}, u32[]{:S(2)}) collective-permute-start(bf16[2,32,256]{2,1,0:T(8,128)(2,1)S(1)} %pad_maximum_fusion.1), channel_id=1, source_target_pairs={{0,2},{1,3},{2,0},{3,1},{4,6},{5,7},{6,4},{7,5},{8,10},{9,11},{10,... | collective-permute-start | bytes 98312 | tf_op jit(solution)/shard_map/ppermute | solution.py:547
  12.0 4.3 %collective-permute-start.2 = (bf16[4,32,256]{2,1,0:T(8,128)(2,1)S(1)}, bf16[4,32,256]{2,1,0:T(8,128)(2,1)S(1)}, u32[]{:S(2)}, u32[]{:S(2)}) collective-permute-start(bf16[4,32,256]{2,1,0:T(8,128)(2,1)S(1)} %pad_maximum_fusion.refs_0_), channel_id=1, source_target_pairs={{0,1},{1,0},{2,3},{3,2},{4,5},{5,4},{6,7},{7,6},{8,9},{9,8},{10,11... | collective-permute-start | bytes 196616 | tf_op jit(solution)/shard_map/ppermute | solution.py:547
  13.5 1.4 %collective-permute-start.4 = (f32[8,256]{1,0:T(8,128)}, f32[8,256]{1,0:T(8,128)S(1)}, u32[]{:S(2)}, u32[]{:S(2)}) collective-permute-start(f32[8,256]{1,0:T(8,128)} %get-tuple-element.35), channel_id=1, source_target_pairs={{0,8},{8,0},{16,24},{24,16},{1,9},{9,1},{17,25},{25,17},{2,10},{10... | collective-permute-start | bytes 24584 | tf_op jit(solution)/shard_map/ppermute | solution.py:580
  14.9 0.7 %copy-start.2 = (f32[8,256]{1,0:T(8,128)S(1)}, f32[8,256]{1,0:T(8,128)}, u32[]{:S(2)}) copy-start(f32[8,256]{1,0:T(8,128)} %get-tuple-element.34.mod_keep_any) | copy-start | bytes 24580
  17.9 5.5 %collective-permute-start.5 = (bf16[256,256]{1,0:T(8,128)(2,1)S(1)}, bf16[256,256]{1,0:T(8,128)(2,1)S(1)}, u32[]{:S(2)}, u32[]{:S(2)}) collective-permute-start(bf16[256,256]{1,0:T(8,128)(2,1)S(1)} %get-tuple-element.40), channel_id=1, source_target_pairs={{0,16},{8,24},{16,0},{24,8},{1,17},{9,25},{17,1},{25,9},{2,18},{10... | collective-permute-start | bytes 393224 | tf_op jit(solution)/shard_map/ppermute | solution.py:595
  23.4 6.5 %collective-permute-start.6 = (bf16[256,256]{1,0:T(8,128)(2,1)S(1)}, bf16[256,256]{1,0:T(8,128)(2,1)S(1)}, u32[]{:S(2)}, u32[]{:S(2)}) collective-permute-start(bf16[256,256]{1,0:T(8,128)(2,1)S(1)} %get-tuple-element.41.grad_ref), channel_id=1, source_target_pairs={{16,0},{24,8},{0,16},{8,24},{17,1},{25,9},{1,17},{9,25},{18,2},{26... | collective-permute-start | bytes 393224 | tf_op jit(solution)/shard_map/ppermute | solution.py:595
  29.9 4.2 %copy-start.1 = (bf16[16,512]{1,0:T(8,128)(2,1)S(1)}, bf16[16,512]{1,0:T(8,128)(2,1)}, u32[]{:S(2)}) copy-start(bf16[16,512]{1,0:T(8,128)(2,1)} %shard_map.121.embedded_hbm.embedded_ref) | copy-start | bytes 49156
  29.9 4.2 %copy-start.3 = (f32[1,256]{1,0:T(1,128)S(1)}, f32[1,256]{1,0:T(1,128)}, u32[]{:S(2)}) copy-start(f32[1,256]{1,0:T(1,128)} %gain_ref.1) | copy-start | bytes 3076
  32.4 1.7 %collective-permute-start.7 = (f32[328,256]{1,0:T(8,128)S(1)}, f32[328,256]{1,0:T(8,128)S(1)}, u32[]{:S(2)}, u32[]{:S(2)}) collective-permute-start(f32[328,256]{1,0:T(8,128)S(1)} %get-tuple-element.51), channel_id=1, source_target_pairs={{0,8},{8,0},{16,24},{24,16},{1,9},{9,1},{17,25},{25,17},{2,10},{10... | collective-permute-start | bytes 1007624 | tf_op jit(solution)/shard_map/ppermute | solution.py:661
where the time goes:
time: 35.9 us; the launch traced here: 35.4 us
  waiting for transfers between devices  11.5 us (32%)
  starting transfers between devices  10.9 us (30%)
  Pallas kernels  10.8 us (30%)
  other arithmetic  0.76 us (2%)
  between operations  0.75 us (2%)
  local copies, waits for them, and re-layouts  0.71 us (2%)
    ppermute x2, waiting for transfers between devices, hop(): return lax.ppermute(value, 'segment', pairs + [(b, a) for a, b in pairs])  7.91 us
    ppermute x3, starting transfers between devices, shards(): far = lax.ppermute(near, 'space', [(i, i ^ bit) for i in range(spaces)])  6.9 us
    ppermute x2, starting transfers between devices, hop(): return lax.ppermute(value, 'segment', pairs + [(b, a) for a, b in pairs])  3.4 us
    pallas_call x1, Pallas kernels, shards(): call(functools.partial(backward_kernel, sh, active), [VMEM] * 10, [pack_s...  2.48 us
    pallas_call x1, Pallas kernels, shards(): call(embed_kernel, [SMEM, SMEM, ANY, ANY], [shape((16, width), bf16)], [p...  2.36 us
    pallas_call x1, Pallas kernels, shards(): call(modulate_kernel, [ANY] * 4, [shape((8, channels), f32)] * 2, [pltpu....  1.88 us
    ppermute x1, waiting for transfers between devices, shards(): other = lax.ppermute(send, 'segment', swap)  1.63 us
    pallas_call x1, Pallas kernels, shards(): call(functools.partial(forward_kernel, sh, 0, (order, far_order)), [VMEM]...  1.58 us
  transfers between devices with their start and end apart: 8, of which 6 were waited for; matrix products, arithmetic and copies ran while one was open for 2% of the time, Pallas kernels for 15%

commit v1 on v0

--- a/solution.py
+++ b/solution.py
@@ -128,7 +128,7 @@
                 part = lax.dot_general(
                     block,
                     weight,
-                    (((1,), (1 if backward else 0,)), ((), ())),
+                    (((1,), (0,)), ((), ())),
                     preferred_element_type=jnp.float32,
                 )
                 total = part if total is None else total + part
@@ -399,7 +399,7 @@
             stats_ref[unit] = stack_rows(*stats)
 
 
-def lay_kernel(sh, active_stage, up_ref, padded_ref):
+def lay_kernel(sh, active_stage, up_ref, weights_ref, padded_ref, turned_ref):
     stage, _ = place_of()
 
     @pl.when(stage == active_stage)
@@ -407,8 +407,13 @@
         clear_edges(sh, padded_ref)
         place_upstream(sh, up_ref, padded_ref)
 
-
-def turn_kernel(sh, active_stage, x_ref, up_ref, laid_ref, params_ref, weights, *refs):
+    for unit in range(PAIR):
+        for tap in range(9):
+            place = slice(tap * sh.channels, (tap + 1) * sh.channels)
+            turned_ref[unit, place, :] = weights_ref[unit, place, :].astype(jnp.float32).T.astype(jnp.bfloat16)
+
+
+def turn_kernel(sh, active_stage, x_ref, up_ref, laid_ref, params_ref, weights, turned, *refs):
     grad_ref, between_ref, act_ref, sums_ref, padded_ref, pre_grad_ref, middle_ref, slope_ref = refs
     stage, _ = place_of()
 
@@ -419,7 +424,7 @@
         acts, slopes = [[ref.at[unit] for unit in range(PAIR)] for ref in (act_ref, slope_ref)]
         first = forward_unit(sh, x_ref, middle_ref, params[0], padded_ref, weights, 0, acts[0], slopes[0])
         second = note_unit(sh, middle_ref, params[1], acts[1], slopes[1])
-        work = (pre_grad_ref, weights)
+        work = (pre_grad_ref, turned)
         known = (slopes[1], second)
         sums_ref[1] = backward_unit(
             sh, middle_ref, up_ref, between_ref, params[1], known, laid_ref, *work, 1, placed=True
@@ -628,18 +633,18 @@
     work = common + [pltpu.VMEM((sh.pixels, channels), f32)]
     slab = [pltpu.VMEM((sh.taps * channels, channels), f32)]
     pair_shape = shape((PAIR, sh.pixels, channels), bf16)
-    (laid,) = call(
+    laid, turned = call(
         functools.partial(lay_kernel, sh, stages - 1),
-        [VMEM],
-        [shape((3, sh.padded, channels), bf16)],
+        [VMEM] * 2,
+        [shape((3, sh.padded, channels), bf16), shape((PAIR, 9 * channels, channels), bf16)],
         cost=some,
-    )(image)
+    )(image, weights)
     *grad, between, act, sums = call(
         functools.partial(turn_kernel, sh, stages - 1),
-        [VMEM] * 5,
+        [VMEM] * 6,
         [image_shape, image_shape, pair_shape, shape((PAIR, 8, channels), f32)],
         work + [pltpu.VMEM((sh.pixels, channels), bf16), pltpu.VMEM((PAIR, sh.pixels, channels), f32)],
-    )(entering[stages - 1], image, laid, params, weights)
+    )(entering[stages - 1], image, laid, params, weights, turned)
     keep, send = call(
         functools.partial(products_kernel, sh, stages - 1),
         [VMEM] * 5,
@@ -657,7 +662,7 @@
             [pack_shape, pack_shape] + ([] if last else [image_shape]),
             (spare if last else []) + work + slab + spare,
             aliases={8: 0, 9: 1},
-        )(entering[active], middles[active], upstream, params, weights, *noted, keep, send)
+        )(entering[active], middles[active], upstream, params, turned, *noted, keep, send)
     other = lax.ppermute(send, "segment", swap)
     finals = [
         ((images, sh.own_rows, channels), bf16),

time: 35.9 us -> 34.5 us (0.961)
  waiting for transfers between devices: 11.5 us -> 10.8 us
  starting transfers between devices: 10.9 us -> 10.3 us
    pallas_call x1, Pallas kernels: 2.48 us -> 1.69 us  [shards(): call(functools.partial(backward_kernel, sh, active), [VMEM] * 10, [pack_s...]
    ppermute x2, waiting for transfers between devices: 7.91 us -> 7.22 us  [hop(): return lax.ppermute(value, 'segment', pairs + [(b, a) for a, b in pairs])]
    pallas_call x2, Pallas kernels: 0.02 us -> 0.7 us  [the longest x1 0.69 us: shards(): call(functools.partial(lay_kernel, sh, stages - 1), [VMEM] * 2, [shape((3...]
    ppermute x2, starting transfers between devices: 3.4 us -> 2.78 us  [hop(): return lax.ppermute(value, 'segment', pairs + [(b, a) for a, b in pairs])]
  transfers between devices with their start and end apart: 8 -> 8, of which waited for: 6 -> 6; matrix products, arithmetic and copies ran while one was open for 2% -> 2% of each run, Pallas kernels for 15% -> 18%
where the time goes in v1:
time: 34.5 us; the launch traced here: 34 us
  waiting for transfers between devices  10.8 us (31%)
  Pallas kernels  10.7 us (31%)
  starting transfers between devices  10.3 us (30%)
  other arithmetic  0.76 us (2%)
  between operations  0.76 us (2%)
  local copies, waits for them, and re-layouts  0.71 us (2%)
    ppermute x2, waiting for transfers between devices, hop(): return lax.ppermute(value, 'segment', pairs + [(b, a) for a, b in pairs])  7.22 us
    ppermute x3, starting transfers between devices, shards(): far = lax.ppermute(near, 'space', [(i, i ^ bit) for i in range(spaces)])  6.9 us
    ppermute x2, starting transfers between devices, hop(): return lax.ppermute(value, 'segment', pairs + [(b, a) for a, b in pairs])  2.78 us
    pallas_call x1, Pallas kernels, shards(): call(embed_kernel, [SMEM, SMEM, ANY, ANY], [shape((16, width), bf16)], [p...  2.36 us
    pallas_call x1, Pallas kernels, shards(): call(modulate_kernel, [ANY] * 4, [shape((8, channels), f32)] * 2, [pltpu....  1.88 us
    pallas_call x1, Pallas kernels, shards(): call(functools.partial(backward_kernel, sh, active), [VMEM] * 10, [pack_s...  1.69 us
    ppermute x1, waiting for transfers between devices, shards(): other = lax.ppermute(send, 'segment', swap)  1.63 us
    pallas_call x1, Pallas kernels, shards(): call(functools.partial(forward_kernel, sh, 0, (order, far_order)), [VMEM]...  1.58 us
  transfers between devices with their start and end apart: 8, of which 6 were waited for; matrix products, arithmetic and copies ran while one was open for 2% of the time, Pallas kernels for 18%

profile of v1, /device:TPU:0, one launch (start us, length us, event | category | flops | bytes accessed | tf_op | source)
XLA Modules:
  0.0 34.0 jit_solution(17638492317750432348)
XLA Ops:
  0.6 0.5 %collective-permute-start.3 = (bf16[2304,256]{1,0:T(8,128)(2,1)}, bf16[2304,256]{1,0:T(8,128)(2,1)S(1)}, u32[]{:S(2)}, u32[]{:S(2)}) collective-permute-start(bf16[2304,256]{1,0:T(8,128)(2,1)} %bitcast.7), channel_id=1, source_target_pairs={{0,8},{8,0},{16,24},{24,16},{1,9},{9,1},{17,25},{25,17},{2,10},{10... | collective-permute-start | bytes 3538952 | tf_op jit(solution)/shard_map/ppermute | solution.py:543
  1.2 0.7 %dynamic-slice_select_fusion = bf16[1,2,16,256]{3,2,1,0:T(8,128)(2,1)S(1)} fusion(bf16[2,2,16,256]{3,2,1,0:T(8,128)(2,1)} %param.11, s32[]{:T(128)S(6)} %select_n.27, bf16[2,2,16,256]{3,2,1,0:T(8,128)(2,1)} %param.10, pred[]{:T(512)S(6)} %eq.5), kind=kLoop, calls=%fused_computation.2 | loop fusion | flops 8192 | bytes 49157 | tf_op jit(solution)/shard_map/jit(_where)/select_n | solution.py:544
  1.9 3.7 %collective-permute-start = (bf16[1,32,256]{2,1,0:T(8,128)(2,1)S(1)}, bf16[1,32,256]{2,1,0:T(8,128)(2,1)S(1)}, u32[]{:S(2)}, u32[]{:S(2)}) collective-permute-start(bf16[1,32,256]{2,1,0:T(8,128)(2,1)S(1)} %bitcast.11), channel_id=1, source_target_pairs={{0,4},{1,5},{2,6},{3,7},{4,0},{5,1},{6,2},{7,3},{8,12},{9,13},{10,... | collective-permute-start | bytes 49160 | tf_op jit(solution)/shard_map/ppermute | solution.py:552
  5.6 2.4 %shard_map.121.embedded_hbm.embedded_ref = bf16[16,512]{1,0:T(8,128)(2,1)} custom-call(s32[2]{0:T(128)} %times_ref.1, s32[2]{0:T(128)} %labels_ref.1, bf16[125,8,512]{2,1,0:T(8,128)(2,1)} %bitcast.9, bf16[128,512]{1,0:T(8,128)(2,1)} %time_weight_hbm.1), custom_call_target="tpu_custom_call" | custom-call | flops 1048576 | bytes 4194304 | tf_op jit(solution)/shard_map/pallas_call | solution.py:554
  8.0 1.6 %collective-permute-start.1 = (bf16[2,32,256]{2,1,0:T(8,128)(2,1)S(1)}, bf16[2,32,256]{2,1,0:T(8,128)(2,1)S(1)}, u32[]{:S(2)}, u32[]{:S(2)}) collective-permute-start(bf16[2,32,256]{2,1,0:T(8,128)(2,1)S(1)} %pad_maximum_fusion.1), channel_id=1, source_target_pairs={{0,2},{1,3},{2,0},{3,1},{4,6},{5,7},{6,4},{7,5},{8,10},{9,11},{10,... | collective-permute-start | bytes 98312 | tf_op jit(solution)/shard_map/ppermute | solution.py:552
  9.6 1.9 %shard_map.122 = (f32[8,256]{1,0:T(8,128)}, f32[8,256]{1,0:T(8,128)}) custom-call(bf16[16,512]{1,0:T(8,128)(2,1)} %shard_map.121.embedded_hbm.embedded_ref, bf16[512,512]{1,0:T(8,128)(2,1)} %bitcast.10, f32[1,512]{1,0:T(1,128)} %bias_hbm.1, f32[1,256]{1,0:T(1,128)} %gain_ref.1), custom_call_target="tpu_custom_call" | custom-call | flops 1048576 | bytes 4194304 | tf_op jit(solution)/shard_map/pallas_call | solution.py:570
  11.5 0.4 %collective-permute-done.1 = bf16[2,32,256]{2,1,0:T(8,128)(2,1)S(1)} collective-permute-done((bf16[2,32,256]{2,1,0:T(8,128)(2,1)S(1)}, bf16[2,32,256]{2,1,0:T(8,128)(2,1)S(1)}, u32[]{:S(2)}, u32[]{:S(2)}) %collective-permute-start.1) | collective-permute-done | bytes 32800 | tf_op jit(solution)/shard_map/ppermute | solution.py:552
  12.0 1.6 %collective-permute-start.2 = (bf16[4,32,256]{2,1,0:T(8,128)(2,1)S(1)}, bf16[4,32,256]{2,1,0:T(8,128)(2,1)S(1)}, u32[]{:S(2)}, u32[]{:S(2)}) collective-permute-start(bf16[4,32,256]{2,1,0:T(8,128)(2,1)S(1)} %pad_maximum_fusion.refs_0_), channel_id=1, source_target_pairs={{0,1},{1,0},{2,3},{3,2},{4,5},{5,4},{6,7},{7,6},{8,9},{9,8},{10,11... | collective-permute-start | bytes 196616 | tf_op jit(solution)/shard_map/ppermute | solution.py:552
  13.5 1.4 %collective-permute-done.4.mod_other_any = f32[8,256]{1,0:T(8,128)S(1)} collective-permute-done((f32[8,256]{1,0:T(8,128)}, f32[8,256]{1,0:T(8,128)S(1)}, u32[]{:S(2)}, u32[]{:S(2)}) %collective-permute-start.4) | collective-permute-done | bytes 8224 | tf_op jit(solution)/shard_map/ppermute | solution.py:585
  14.9 0.7 %copy-done.2 = f32[8,256]{1,0:T(8,128)S(1)} copy-done((f32[8,256]{1,0:T(8,128)S(1)}, f32[8,256]{1,0:T(8,128)}, u32[]{:S(2)}) %copy-start.2) | copy-done | bytes 8216
  15.6 0.5 %shard_map.123 = (bf16[2,2304,256]{2,1,0:T(8,128)(2,1)S(1)}, f32[8,256]{1,0:T(8,128)S(1)}) custom-call(bf16[2304,256]{1,0:T(8,128)(2,1)S(1)} %bitcast.8, bf16[2304,256]{1,0:T(8,128)(2,1)S(1)} %collective-permute-done.3.other_any, f32[8,256]{1,0:T(8,128)S(1)} %copy-done.2, f32[8,256]{1,0:T(8,128)S(1)} %collective-permute-done.4.mod_other_any), custom_call_target="tpu_custom_call" | custom-call | flops 1048576 | bytes 4194304 | tf_op jit(solution)/shard_map/pallas_call | solution.py:586
  16.2 0.2 collective-permute-done.2.refs_1_
  16.3 1.6 %shard_map.124 = (bf16[256,256]{1,0:T(8,128)(2,1)S(1)}, bf16[256,256]{1,0:T(8,128)(2,1)S(1)}, bf16[256,256]{1,0:T(8,128)(2,1)S(1)}) custom-call(bf16[4,32,256]{2,1,0:T(8,128)(2,1)S(1)} %pad_maximum_fusion.refs_0_, bf16[4,32,256]{2,1,0:T(8,128)(2,1)S(1)} %collective-permute-done.2.refs_1_, f32[8,256]{1,0:T(8,128)S(1)} %get-tuple-element.38.refs_2_.params_ref.refs_3_, ...), custom_call_target="tpu_custom_call" | custom-call | tf_op jit(solution)/shard_map/pallas_call | solution.py:602
  17.9 0.1 collective-permute-start.5
  18.0 0.7 %shard_map.125 = (bf16[3,288,256]{2,1,0:T(8,128)(2,1)S(1)}, bf16[2,2304,256]{2,1,0:T(8,128)(2,1)S(1)}) custom-call(bf16[256,256]{1,0:T(8,128)(2,1)S(1)} %get-tuple-element.40.up_ref.x_ref.refs_0_, bf16[2,2304,256]{2,1,0:T(8,128)(2,1)S(1)} %get-tuple-element.39.refs_3_.weights_ref.weights), custom_call_target="tpu_custom_call" | custom-call | flops 1048576 | bytes 4194304 | tf_op jit(solution)/shard_map/pallas_call | solution.py:636
  18.7 4.7 %collective-permute-done.5.x_ref = bf16[256,256]{1,0:T(8,128)(2,1)S(1)} collective-permute-done((bf16[256,256]{1,0:T(8,128)(2,1)S(1)}, bf16[256,256]{1,0:T(8,128)(2,1)S(1)}, u32[]{:S(2)}, u32[]{:S(2)}) %collective-permute-start.5) | collective-permute-done | bytes 131104 | tf_op jit(solution)/shard_map/ppermute | solution.py:600
  23.4 2.7 %collective-permute-start.6 = (bf16[256,256]{1,0:T(8,128)(2,1)S(1)}, bf16[256,256]{1,0:T(8,128)(2,1)S(1)}, u32[]{:S(2)}, u32[]{:S(2)}) collective-permute-start(bf16[256,256]{1,0:T(8,128)(2,1)S(1)} %get-tuple-element.45.grad_ref), channel_id=1, source_target_pairs={{16,0},{24,8},{0,16},{8,24},{17,1},{25,9},{1,17},{9,25},{18,2},{26... | collective-permute-start | bytes 393224 | tf_op jit(solution)/shard_map/ppermute | solution.py:600
  26.1 0.6 %shard_map.127 = (bf16[2,256,256]{2,1,0:T(8,128)(2,1)S(1)}, f32[2,256,256]{2,1,0:T(8,128)S(1)}, f32[2,8,256]{2,1,0:T(8,128)S(1)}) custom-call(bf16[256,256]{1,0:T(8,128)(2,1)S(1)} %get-tuple-element.40.up_ref.x_ref.refs_0_, bf16[256,256]{1,0:T(8,128)(2,1)S(1)} %get-tuple-element.41.middle_ref.refs_1_, f32[8,256]{1,0:T(8,128)S(1)} %get-tuple-element.38.refs_2_.params_ref.refs_3_), custom_call_target="tpu_custom_call" | custom-call | flops 1048576 | bytes 4194304 | tf_op jit(solution)/shard_map/pallas_call | solution.py:621
  26.8 0.0 copy-start.1
  26.8 2.5 %collective-permute-done.6.refs_2_ = bf16[256,256]{1,0:T(8,128)(2,1)S(1)} collective-permute-done((bf16[256,256]{1,0:T(8,128)(2,1)S(1)}, bf16[256,256]{1,0:T(8,128)(2,1)S(1)}, u32[]{:S(2)}, u32[]{:S(2)}) %collective-permute-start.6) | collective-permute-done | bytes 131104 | tf_op jit(solution)/shard_map/ppermute | solution.py:600
  29.3 1.7 %shard_map.129 = (f32[328,256]{1,0:T(8,128)S(1)}, f32[328,256]{1,0:T(8,128)S(1)}) custom-call(bf16[256,256]{1,0:T(8,128)(2,1)S(1)} %get-tuple-element.40.up_ref.x_ref.refs_0_, bf16[256,256]{1,0:T(8,128)(2,1)S(1)} %get-tuple-element.41.middle_ref.refs_1_, ...), custom_call_target="tpu_custom_call", output_to_operand_aliasing={{0}: (8, {}), {1}: (9, {})} | custom-call | tf_op jit(solution)/shard_map/pallas_call | solution.py:659
  31.0 0.1 collective-permute-start.7
  31.1 1.6 %collective-permute-done.7.other_ref = f32[328,256]{1,0:T(8,128)S(1)} collective-permute-done((f32[328,256]{1,0:T(8,128)S(1)}, f32[328,256]{1,0:T(8,128)S(1)}, u32[]{:S(2)}, u32[]{:S(2)}) %collective-permute-start.7) | collective-permute-done | bytes 335904 | tf_op jit(solution)/shard_map/ppermute | solution.py:666
  32.7 1.3 %shard_map.130 = (bf16[2,32,256]{2,1,0:T(8,128)(2,1)}, f32[288,256]{1,0:T(8,128)}, f32[512,512]{1,0:T(8,128)}) custom-call(f32[328,256]{1,0:T(8,128)S(1)} %get-tuple-element.54.keep_ref, f32[328,256]{1,0:T(8,128)S(1)} %collective-permute-done.7.other_ref, bf16[16,512]{1,0:T(8,128)(2,1)S(1)} %copy-done.1, f32[1,256]{1,0:T(1,128)S(1)} %copy-done.3), custom_call_target="tpu_custom_call" | custom-call | tf_op jit(solution)/shard_map/pallas_call | solution.py:672
  (13 shorter events, 0.1 us)
Async XLA Ops:
  0.6 14.3 %copy-start = (bf16[1,3,3,256,256]{4,3,2,1,0:T(8,128)(2,1)S(1)}, bf16[1,3,3,256,256]{4,3,2,1,0:T(8,128)(2,1)}, u32[]{:S(2)}) copy-start(bf16[1,3,3,256,256]{4,3,2,1,0:T(8,128)(2,1)} %param.16) | copy-start | bytes 3538948
  0.6 14.3 %collective-permute-start.3 = (bf16[2304,256]{1,0:T(8,128)(2,1)}, bf16[2304,256]{1,0:T(8,128)(2,1)S(1)}, u32[]{:S(2)}, u32[]{:S(2)}) collective-permute-start(bf16[2304,256]{1,0:T(8,128)(2,1)} %bitcast.7), channel_id=1, source_target_pairs={{0,8},{8,0},{16,24},{24,16},{1,9},{9,1},{17,25},{25,17},{2,10},{10... | collective-permute-start | bytes 3538952 | tf_op jit(solution)/shard_map/ppermute | solution.py:543
  1.9 6.1 %collective-permute-start = (bf16[1,32,256]{2,1,0:T(8,128)(2,1)S(1)}, bf16[1,32,256]{2,1,0:T(8,128)(2,1)S(1)}, u32[]{:S(2)}, u32[]{:S(2)}) collective-permute-start(bf16[1,32,256]{2,1,0:T(8,128)(2,1)S(1)} %bitcast.11), channel_id=1, source_target_pairs={{0,4},{1,5},{2,6},{3,7},{4,0},{5,1},{6,2},{7,3},{8,12},{9,13},{10,... | collective-permute-start | bytes 49160 | tf_op jit(solution)/shard_map/ppermute | solution.py:552
  8.0 4.0 %collective-permute-start.1 = (bf16[2,32,256]{2,1,0:T(8,128)(2,1)S(1)}, bf16[2,32,256]{2,1,0:T(8,128)(2,1)S(1)}, u32[]{:S(2)}, u32[]{:S(2)}) collective-permute-start(bf16[2,32,256]{2,1,0:T(8,128)(2,1)S(1)} %pad_maximum_fusion.1), channel_id=1, source_target_pairs={{0,2},{1,3},{2,0},{3,1},{4,6},{5,7},{6,4},{7,5},{8,10},{9,11},{10,... | collective-permute-start | bytes 98312 | tf_op jit(solution)/shard_map/ppermute | solution.py:552
  12.0 4.3 %collective-permute-start.2 = (bf16[4,32,256]{2,1,0:T(8,128)(2,1)S(1)}, bf16[4,32,256]{2,1,0:T(8,128)(2,1)S(1)}, u32[]{:S(2)}, u32[]{:S(2)}) collective-permute-start(bf16[4,32,256]{2,1,0:T(8,128)(2,1)S(1)} %pad_maximum_fusion.refs_0_), channel_id=1, source_target_pairs={{0,1},{1,0},{2,3},{3,2},{4,5},{5,4},{6,7},{7,6},{8,9},{9,8},{10,11... | collective-permute-start | bytes 196616 | tf_op jit(solution)/shard_map/ppermute | solution.py:552
  13.5 1.4 %collective-permute-start.4 = (f32[8,256]{1,0:T(8,128)}, f32[8,256]{1,0:T(8,128)S(1)}, u32[]{:S(2)}, u32[]{:S(2)}) collective-permute-start(f32[8,256]{1,0:T(8,128)} %get-tuple-element.37), channel_id=1, source_target_pairs={{0,8},{8,0},{16,24},{24,16},{1,9},{9,1},{17,25},{25,17},{2,10},{10... | collective-permute-start | bytes 24584 | tf_op jit(solution)/shard_map/ppermute | solution.py:585
  14.9 0.7 %copy-start.2 = (f32[8,256]{1,0:T(8,128)S(1)}, f32[8,256]{1,0:T(8,128)}, u32[]{:S(2)}) copy-start(f32[8,256]{1,0:T(8,128)} %get-tuple-element.36.mod_keep_any) | copy-start | bytes 24580
  17.9 5.5 %collective-permute-start.5 = (bf16[256,256]{1,0:T(8,128)(2,1)S(1)}, bf16[256,256]{1,0:T(8,128)(2,1)S(1)}, u32[]{:S(2)}, u32[]{:S(2)}) collective-permute-start(bf16[256,256]{1,0:T(8,128)(2,1)S(1)} %get-tuple-element.42), channel_id=1, source_target_pairs={{0,16},{8,24},{16,0},{24,8},{1,17},{9,25},{17,1},{25,9},{2,18},{10... | collective-permute-start | bytes 393224 | tf_op jit(solution)/shard_map/ppermute | solution.py:600
  23.4 5.9 %collective-permute-start.6 = (bf16[256,256]{1,0:T(8,128)(2,1)S(1)}, bf16[256,256]{1,0:T(8,128)(2,1)S(1)}, u32[]{:S(2)}, u32[]{:S(2)}) collective-permute-start(bf16[256,256]{1,0:T(8,128)(2,1)S(1)} %get-tuple-element.45.grad_ref), channel_id=1, source_target_pairs={{16,0},{24,8},{0,16},{8,24},{17,1},{25,9},{1,17},{9,25},{18,2},{26... | collective-permute-start | bytes 393224 | tf_op jit(solution)/shard_map/ppermute | solution.py:600
  26.8 5.9 %copy-start.1 = (bf16[16,512]{1,0:T(8,128)(2,1)S(1)}, bf16[16,512]{1,0:T(8,128)(2,1)}, u32[]{:S(2)}) copy-start(bf16[16,512]{1,0:T(8,128)(2,1)} %shard_map.121.embedded_hbm.embedded_ref) | copy-start | bytes 49156
  26.8 5.9 %copy-start.3 = (f32[1,256]{1,0:T(1,128)S(1)}, f32[1,256]{1,0:T(1,128)}, u32[]{:S(2)}) copy-start(f32[1,256]{1,0:T(1,128)} %gain_ref.1) | copy-start | bytes 3076
  31.0 1.7 %collective-permute-start.7 = (f32[328,256]{1,0:T(8,128)S(1)}, f32[328,256]{1,0:T(8,128)S(1)}, u32[]{:S(2)}, u32[]{:S(2)}) collective-permute-start(f32[328,256]{1,0:T(8,128)S(1)} %get-tuple-element.55), channel_id=1, source_target_pairs={{0,8},{8,0},{16,24},{24,16},{1,9},{9,1},{17,25},{25,17},{2,10},{10... | collective-permute-start | bytes 1007624 | tf_op jit(solution)/shard_map/ppermute | solution.py:666

commit v2 on v1

--- a/solution.py
+++ b/solution.py
@@ -11,7 +11,7 @@
 GROUPS = 32
 EPSILON = 1e-05
 PAIR = 2
-BLOCK = 128
+BLOCK = 64
 MOD_PARTS = 4
 PREPARE_LIMIT = 60 << 20
 CHAIN_LIMIT = 48 << 20
@@ -312,7 +312,8 @@
     return copies
 
 
-def embed_kernel(times_ref, labels_ref, table_hbm, time_weight_hbm, embedded_ref, table_ref, time_weight_ref, sems):
+def embed_kernel(times_ref, labels_ref, table_hbm, time_weight_hbm, *refs):
+    embedded_ref, turned_ref, table_ref, time_weight_ref, sems = refs
     pairs = [(time_weight_hbm, time_weight_ref)]
     pairs += [(table_hbm.at[pl.ds(labels_ref[i] // 8, 1)], table_ref.at[pl.ds(i, 1)]) for i in range(PAIR)]
     copies = start_all(pairs, sems)
@@ -329,7 +330,9 @@
         copy.wait()
     timed = jnp.dot(sinusoid, time_weight_ref[...], preferred_element_type=jnp.float32)
     timed = timed + jnp.where(spot % 2 == 0, label_row(0), label_row(1))
-    embedded_ref[...] = (timed * sigmoid(timed)).astype(jnp.bfloat16)
+    embedded = timed * sigmoid(timed)
+    embedded_ref[...] = embedded.astype(jnp.bfloat16)
+    turned_ref[...] = embedded.T.astype(jnp.bfloat16)
 
 
 def modulate_kernel(embedded_hbm, mod_weight_hbm, bias_hbm, gain_hbm, keep_ref, send_ref, *scratch):
@@ -487,9 +490,9 @@
     for k in range(MOD_PARTS):
         place = slice(k * size, (k + 1) * size)
         mod_ref[place, :] = lax.dot_general(
-            embedded_ref[:, place],
+            embedded_ref[place, :],
             pieces,
-            (((0,), (0,)), ((), ())),
+            (((1,), (0,)), ((), ())),
             preferred_element_type=jnp.float32,
         )
         copies.append(pltpu.make_async_copy(mod_ref.at[place], mod_hbm.at[place], sems.at[k]))
@@ -551,10 +554,10 @@
     while True:
         far = lax.ppermute(near, "space", [(i, i ^ bit) for i in range(spaces)])
         if not waiting:
-            (embedded,) = call(
+            embedded, turned_embedded = call(
                 embed_kernel,
                 [SMEM, SMEM, ANY, ANY],
-                [shape((16, width), bf16)],
+                [shape((16, width), bf16), shape((width, 16), bf16)],
                 [
                     pltpu.VMEM((PAIR, 8, width), bf16),
                     pltpu.VMEM(time_weight.shape, bf16),
@@ -676,7 +679,7 @@
         out_specs=[ANY] * 3,
         scratch_shapes=[pltpu.VMEM(*final) for final in finals] + [pltpu.SemaphoreType.DMA((MOD_PARTS + 2,))],
         compiler_params=pltpu.CompilerParams(vmem_limit_bytes=CHAIN_LIMIT),
-    )(keep, other, embedded, norm_gain)
+    )(keep, other, turned_embedded, norm_gain)
     return (grads.reshape(1, images, row_count, cols, channels), conv_grad[None], mod_grad[None])
 
 

time: 34.5 us -> 37.1 us (1.075)
  Pallas kernels: 10.7 us -> 12.2 us
  starting transfers between devices: 10.3 us -> 11.4 us
    ppermute x2, starting transfers between devices: 2.78 us -> 3.92 us  [hop(): return lax.ppermute(value, 'segment', pairs + [(b, a) for a, b in pairs])]
    pallas_call x1, Pallas kernels: 1.69 us -> 2.53 us  [shards(): call(functools.partial(backward_kernel, sh, active), [VMEM] * 10, [pack_s...]
    pallas_call x1, Pallas kernels: 1.58 us -> 2.14 us  [shards(): call(functools.partial(forward_kernel, sh, 0, (order, far_order)), [VMEM]...]
  transfers between devices with their start and end apart: 8 -> 8, of which waited for: 6 -> 6; matrix products, arithmetic and copies ran while one was open for 2% -> 2% of each run, Pallas kernels for 18% -> 17%
where the time goes in v2:
time: 37.1 us; the launch traced here: 36.7 us
  Pallas kernels  12.2 us (33%)
  starting transfers between devices  11.4 us (31%)
  waiting for transfers between devices  10.8 us (29%)
  other arithmetic  0.76 us (2%)
  between operations  0.76 us (2%)
  local copies, waits for them, and re-layouts  0.71 us (2%)
    ppermute x2, waiting for transfers between devices, hop(): return lax.ppermute(value, 'segment', pairs + [(b, a) for a, b in pairs])  7.21 us
    ppermute x3, starting transfers between devices, shards(): far = lax.ppermute(near, 'space', [(i, i ^ bit) for i in range(spaces)])  6.9 us
    ppermute x2, starting transfers between devices, hop(): return lax.ppermute(value, 'segment', pairs + [(b, a) for a, b in pairs])  3.92 us
    pallas_call x1, Pallas kernels, shards(): call(functools.partial(backward_kernel, sh, active), [VMEM] * 10, [pack_s...  2.53 us
    pallas_call x1, Pallas kernels, shards(): call(embed_kernel, [SMEM, SMEM, ANY, ANY], [shape((16, width), bf16), sha...  2.51 us
    pallas_call x1, Pallas kernels, shards(): call(functools.partial(forward_kernel, sh, 0, (order, far_order)), [VMEM]...  2.14 us
    pallas_call x1, Pallas kernels, shards(): call(modulate_kernel, [ANY] * 4, [shape((8, channels), f32)] * 2, [pltpu....  1.88 us
    ppermute x1, waiting for transfers between devices, shards(): other = lax.ppermute(send, 'segment', swap)  1.63 us
  transfers between devices with their start and end apart: 8, of which 6 were waited for; matrix products, arithmetic and copies ran while one was open for 2% of the time, Pallas kernels for 17%

profile of v2, /device:TPU:0, one launch (start us, length us, event | category | flops | bytes accessed | tf_op | source)
XLA Modules:
  0.0 36.7 jit_solution(17350851805703043552)
XLA Ops:
  0.6 0.5 %collective-permute-start.3 = (bf16[2304,256]{1,0:T(8,128)(2,1)}, bf16[2304,256]{1,0:T(8,128)(2,1)S(1)}, u32[]{:S(2)}, u32[]{:S(2)}) collective-permute-start(bf16[2304,256]{1,0:T(8,128)(2,1)} %bitcast.7), channel_id=1, source_target_pairs={{0,8},{8,0},{16,24},{24,16},{1,9},{9,1},{17,25},{25,17},{2,10},{10... | collective-permute-start | bytes 3538952 | tf_op jit(solution)/shard_map/ppermute | solution.py:546
  1.2 0.7 %dynamic-slice_select_fusion = bf16[1,2,16,256]{3,2,1,0:T(8,128)(2,1)S(1)} fusion(bf16[2,2,16,256]{3,2,1,0:T(8,128)(2,1)} %param.11, s32[]{:T(128)S(6)} %select_n.27, bf16[2,2,16,256]{3,2,1,0:T(8,128)(2,1)} %param.10, pred[]{:T(512)S(6)} %eq.5), kind=kLoop, calls=%fused_computation.2 | loop fusion | flops 8192 | bytes 49157 | tf_op jit(solution)/shard_map/jit(_where)/select_n | solution.py:547
  1.9 3.7 %collective-permute-start = (bf16[1,32,256]{2,1,0:T(8,128)(2,1)S(1)}, bf16[1,32,256]{2,1,0:T(8,128)(2,1)S(1)}, u32[]{:S(2)}, u32[]{:S(2)}) collective-permute-start(bf16[1,32,256]{2,1,0:T(8,128)(2,1)S(1)} %bitcast.11), channel_id=1, source_target_pairs={{0,4},{1,5},{2,6},{3,7},{4,0},{5,1},{6,2},{7,3},{8,12},{9,13},{10,... | collective-permute-start | bytes 49160 | tf_op jit(solution)/shard_map/ppermute | solution.py:555
  5.6 2.5 %shard_map.121 = (bf16[16,512]{1,0:T(8,128)(2,1)}, bf16[512,16]{1,0:T(8,128)(2,1)}) custom-call(s32[2]{0:T(128)} %times_ref.1, s32[2]{0:T(128)} %labels_ref.1, bf16[125,8,512]{2,1,0:T(8,128)(2,1)} %bitcast.9, bf16[128,512]{1,0:T(8,128)(2,1)} %time_weight_hbm.1), custom_call_target="tpu_custom_call" | custom-call | flops 1048576 | bytes 4194304 | tf_op jit(solution)/shard_map/pallas_call | solution.py:557
  8.1 1.6 %collective-permute-start.1 = (bf16[2,32,256]{2,1,0:T(8,128)(2,1)S(1)}, bf16[2,32,256]{2,1,0:T(8,128)(2,1)S(1)}, u32[]{:S(2)}, u32[]{:S(2)}) collective-permute-start(bf16[2,32,256]{2,1,0:T(8,128)(2,1)S(1)} %pad_maximum_fusion.1), channel_id=1, source_target_pairs={{0,2},{1,3},{2,0},{3,1},{4,6},{5,7},{6,4},{7,5},{8,10},{9,11},{10,... | collective-permute-start | bytes 98312 | tf_op jit(solution)/shard_map/ppermute | solution.py:555
  9.8 1.9 %shard_map.122 = (f32[8,256]{1,0:T(8,128)}, f32[8,256]{1,0:T(8,128)}) custom-call(bf16[16,512]{1,0:T(8,128)(2,1)} %get-tuple-element.35.embedded_hbm, bf16[512,512]{1,0:T(8,128)(2,1)} %bitcast.10, f32[1,512]{1,0:T(1,128)} %bias_hbm.1, f32[1,256]{1,0:T(1,128)} %gain_ref.1), custom_call_target="tpu_custom_call" | custom-call | flops 1048576 | bytes 4194304 | tf_op jit(solution)/shard_map/pallas_call | solution.py:573
  11.7 0.4 %collective-permute-done.1 = bf16[2,32,256]{2,1,0:T(8,128)(2,1)S(1)} collective-permute-done((bf16[2,32,256]{2,1,0:T(8,128)(2,1)S(1)}, bf16[2,32,256]{2,1,0:T(8,128)(2,1)S(1)}, u32[]{:S(2)}, u32[]{:S(2)}) %collective-permute-start.1) | collective-permute-done | bytes 32800 | tf_op jit(solution)/shard_map/ppermute | solution.py:555
  12.1 1.6 %collective-permute-start.2 = (bf16[4,32,256]{2,1,0:T(8,128)(2,1)S(1)}, bf16[4,32,256]{2,1,0:T(8,128)(2,1)S(1)}, u32[]{:S(2)}, u32[]{:S(2)}) collective-permute-start(bf16[4,32,256]{2,1,0:T(8,128)(2,1)S(1)} %pad_maximum_fusion.refs_0_), channel_id=1, source_target_pairs={{0,1},{1,0},{2,3},{3,2},{4,5},{5,4},{6,7},{7,6},{8,9},{9,8},{10,11... | collective-permute-start | bytes 196616 | tf_op jit(solution)/shard_map/ppermute | solution.py:555
  13.7 1.4 %collective-permute-done.4.mod_other_any = f32[8,256]{1,0:T(8,128)S(1)} collective-permute-done((f32[8,256]{1,0:T(8,128)}, f32[8,256]{1,0:T(8,128)S(1)}, u32[]{:S(2)}, u32[]{:S(2)}) %collective-permute-start.4) | collective-permute-done | bytes 8224 | tf_op jit(solution)/shard_map/ppermute | solution.py:588
  15.1 0.7 %copy-done.2 = f32[8,256]{1,0:T(8,128)S(1)} copy-done((f32[8,256]{1,0:T(8,128)S(1)}, f32[8,256]{1,0:T(8,128)}, u32[]{:S(2)}) %copy-start.2) | copy-done | bytes 8216
  15.8 0.5 %shard_map.123 = (bf16[2,2304,256]{2,1,0:T(8,128)(2,1)S(1)}, f32[8,256]{1,0:T(8,128)S(1)}) custom-call(bf16[2304,256]{1,0:T(8,128)(2,1)S(1)} %bitcast.8, bf16[2304,256]{1,0:T(8,128)(2,1)S(1)} %collective-permute-done.3.other_any, f32[8,256]{1,0:T(8,128)S(1)} %copy-done.2, f32[8,256]{1,0:T(8,128)S(1)} %collective-permute-done.4.mod_other_any), custom_call_target="tpu_custom_call" | custom-call | flops 1048576 | bytes 4194304 | tf_op jit(solution)/shard_map/pallas_call | solution.py:589
  16.3 0.2 collective-permute-done.2.refs_1_
  16.5 2.1 %shard_map.124 = (bf16[256,256]{1,0:T(8,128)(2,1)S(1)}, bf16[256,256]{1,0:T(8,128)(2,1)S(1)}, bf16[256,256]{1,0:T(8,128)(2,1)S(1)}) custom-call(bf16[4,32,256]{2,1,0:T(8,128)(2,1)S(1)} %pad_maximum_fusion.refs_0_, bf16[4,32,256]{2,1,0:T(8,128)(2,1)S(1)} %collective-permute-done.2.refs_1_, f32[8,256]{1,0:T(8,128)S(1)} %get-tuple-element.41.refs_2_.params_ref.refs_3_, ...), custom_call_target="tpu_custom_call" | custom-call | tf_op jit(solution)/shard_map/pallas_call | solution.py:605
  18.6 0.1 collective-permute-start.5
  18.7 0.7 %shard_map.125 = (bf16[3,288,256]{2,1,0:T(8,128)(2,1)S(1)}, bf16[2,2304,256]{2,1,0:T(8,128)(2,1)S(1)}) custom-call(bf16[256,256]{1,0:T(8,128)(2,1)S(1)} %get-tuple-element.43.up_ref.x_ref.refs_0_, bf16[2,2304,256]{2,1,0:T(8,128)(2,1)S(1)} %get-tuple-element.42.refs_3_.weights_ref.weights), custom_call_target="tpu_custom_call" | custom-call | flops 1048576 | bytes 4194304 | tf_op jit(solution)/shard_map/pallas_call | solution.py:639
  19.4 4.7 %collective-permute-done.5.x_ref = bf16[256,256]{1,0:T(8,128)(2,1)S(1)} collective-permute-done((bf16[256,256]{1,0:T(8,128)(2,1)S(1)}, bf16[256,256]{1,0:T(8,128)(2,1)S(1)}, u32[]{:S(2)}, u32[]{:S(2)}) %collective-permute-start.5) | collective-permute-done | bytes 131104 | tf_op jit(solution)/shard_map/ppermute | solution.py:603
  24.1 3.8 %collective-permute-start.6 = (bf16[256,256]{1,0:T(8,128)(2,1)S(1)}, bf16[256,256]{1,0:T(8,128)(2,1)S(1)}, u32[]{:S(2)}, u32[]{:S(2)}) collective-permute-start(bf16[256,256]{1,0:T(8,128)(2,1)S(1)} %get-tuple-element.48.grad_ref), channel_id=1, source_target_pairs={{16,0},{24,8},{0,16},{8,24},{17,1},{25,9},{1,17},{9,25},{18,2},{26... | collective-permute-start | bytes 393224 | tf_op jit(solution)/shard_map/ppermute | solution.py:603
  28.0 0.6 %shard_map.127 = (bf16[2,256,256]{2,1,0:T(8,128)(2,1)S(1)}, f32[2,256,256]{2,1,0:T(8,128)S(1)}, f32[2,8,256]{2,1,0:T(8,128)S(1)}) custom-call(bf16[256,256]{1,0:T(8,128)(2,1)S(1)} %get-tuple-element.43.up_ref.x_ref.refs_0_, bf16[256,256]{1,0:T(8,128)(2,1)S(1)} %get-tuple-element.44.middle_ref.refs_1_, f32[8,256]{1,0:T(8,128)S(1)} %get-tuple-element.41.refs_2_.params_ref.refs_3_), custom_call_target="tpu_custom_call" | custom-call | flops 1048576 | bytes 4194304 | tf_op jit(solution)/shard_map/pallas_call | solution.py:624
  28.6 0.0 copy-start.1
  28.7 2.5 %collective-permute-done.6.refs_2_ = bf16[256,256]{1,0:T(8,128)(2,1)S(1)} collective-permute-done((bf16[256,256]{1,0:T(8,128)(2,1)S(1)}, bf16[256,256]{1,0:T(8,128)(2,1)S(1)}, u32[]{:S(2)}, u32[]{:S(2)}) %collective-permute-start.6) | collective-permute-done | bytes 131104 | tf_op jit(solution)/shard_map/ppermute | solution.py:603
  31.1 2.5 %shard_map.129 = (f32[328,256]{1,0:T(8,128)S(1)}, f32[328,256]{1,0:T(8,128)S(1)}) custom-call(bf16[256,256]{1,0:T(8,128)(2,1)S(1)} %get-tuple-element.43.up_ref.x_ref.refs_0_, bf16[256,256]{1,0:T(8,128)(2,1)S(1)} %get-tuple-element.44.middle_ref.refs_1_, ...), custom_call_target="tpu_custom_call", output_to_operand_aliasing={{0}: (8, {}), {1}: (9, {})} | custom-call | tf_op jit(solution)/shard_map/pallas_call | solution.py:662
  33.7 0.1 collective-permute-start.7
  33.7 1.6 %collective-permute-done.7.other_ref = f32[328,256]{1,0:T(8,128)S(1)} collective-permute-done((f32[328,256]{1,0:T(8,128)S(1)}, f32[328,256]{1,0:T(8,128)S(1)}, u32[]{:S(2)}, u32[]{:S(2)}) %collective-permute-start.7) | collective-permute-done | bytes 335904 | tf_op jit(solution)/shard_map/ppermute | solution.py:669
  35.4 1.3 %shard_map.130 = (bf16[2,32,256]{2,1,0:T(8,128)(2,1)}, f32[288,256]{1,0:T(8,128)}, f32[512,512]{1,0:T(8,128)}) custom-call(f32[328,256]{1,0:T(8,128)S(1)} %get-tuple-element.57.keep_ref, f32[328,256]{1,0:T(8,128)S(1)} %collective-permute-done.7.other_ref, bf16[512,16]{1,0:T(8,128)(2,1)S(1)} %copy-done.1, f32[1,256]{1,0:T(1,128)S(1)} %copy-done.3), custom_call_target="tpu_custom_call" | custom-call | tf_op jit(solution)/shard_map/pallas_call | solution.py:675
  (13 shorter events, 0.1 us)
Async XLA Ops:
  0.6 14.5 %copy-start = (bf16[1,3,3,256,256]{4,3,2,1,0:T(8,128)(2,1)S(1)}, bf16[1,3,3,256,256]{4,3,2,1,0:T(8,128)(2,1)}, u32[]{:S(2)}) copy-start(bf16[1,3,3,256,256]{4,3,2,1,0:T(8,128)(2,1)} %param.16) | copy-start | bytes 3538948
  0.6 14.4 %collective-permute-start.3 = (bf16[2304,256]{1,0:T(8,128)(2,1)}, bf16[2304,256]{1,0:T(8,128)(2,1)S(1)}, u32[]{:S(2)}, u32[]{:S(2)}) collective-permute-start(bf16[2304,256]{1,0:T(8,128)(2,1)} %bitcast.7), channel_id=1, source_target_pairs={{0,8},{8,0},{16,24},{24,16},{1,9},{9,1},{17,25},{25,17},{2,10},{10... | collective-permute-start | bytes 3538952 | tf_op jit(solution)/shard_map/ppermute | solution.py:546
  1.9 6.2 %collective-permute-start = (bf16[1,32,256]{2,1,0:T(8,128)(2,1)S(1)}, bf16[1,32,256]{2,1,0:T(8,128)(2,1)S(1)}, u32[]{:S(2)}, u32[]{:S(2)}) collective-permute-start(bf16[1,32,256]{2,1,0:T(8,128)(2,1)S(1)} %bitcast.11), channel_id=1, source_target_pairs={{0,4},{1,5},{2,6},{3,7},{4,0},{5,1},{6,2},{7,3},{8,12},{9,13},{10,... | collective-permute-start | bytes 49160 | tf_op jit(solution)/shard_map/ppermute | solution.py:555
  8.1 4.0 %collective-permute-start.1 = (bf16[2,32,256]{2,1,0:T(8,128)(2,1)S(1)}, bf16[2,32,256]{2,1,0:T(8,128)(2,1)S(1)}, u32[]{:S(2)}, u32[]{:S(2)}) collective-permute-start(bf16[2,32,256]{2,1,0:T(8,128)(2,1)S(1)} %pad_maximum_fusion.1), channel_id=1, source_target_pairs={{0,2},{1,3},{2,0},{3,1},{4,6},{5,7},{6,4},{7,5},{8,10},{9,11},{10,... | collective-permute-start | bytes 98312 | tf_op jit(solution)/shard_map/ppermute | solution.py:555
  12.1 4.3 %collective-permute-start.2 = (bf16[4,32,256]{2,1,0:T(8,128)(2,1)S(1)}, bf16[4,32,256]{2,1,0:T(8,128)(2,1)S(1)}, u32[]{:S(2)}, u32[]{:S(2)}) collective-permute-start(bf16[4,32,256]{2,1,0:T(8,128)(2,1)S(1)} %pad_maximum_fusion.refs_0_), channel_id=1, source_target_pairs={{0,1},{1,0},{2,3},{3,2},{4,5},{5,4},{6,7},{7,6},{8,9},{9,8},{10,11... | collective-permute-start | bytes 196616 | tf_op jit(solution)/shard_map/ppermute | solution.py:555
  13.7 1.4 %collective-permute-start.4 = (f32[8,256]{1,0:T(8,128)}, f32[8,256]{1,0:T(8,128)S(1)}, u32[]{:S(2)}, u32[]{:S(2)}) collective-permute-start(f32[8,256]{1,0:T(8,128)} %get-tuple-element.40), channel_id=1, source_target_pairs={{0,8},{8,0},{16,24},{24,16},{1,9},{9,1},{17,25},{25,17},{2,10},{10... | collective-permute-start | bytes 24584 | tf_op jit(solution)/shard_map/ppermute | solution.py:588
  15.1 0.7 %copy-start.2 = (f32[8,256]{1,0:T(8,128)S(1)}, f32[8,256]{1,0:T(8,128)}, u32[]{:S(2)}) copy-start(f32[8,256]{1,0:T(8,128)} %get-tuple-element.39.mod_keep_any) | copy-start | bytes 24580
  18.6 5.5 %collective-permute-start.5 = (bf16[256,256]{1,0:T(8,128)(2,1)S(1)}, bf16[256,256]{1,0:T(8,128)(2,1)S(1)}, u32[]{:S(2)}, u32[]{:S(2)}) collective-permute-start(bf16[256,256]{1,0:T(8,128)(2,1)S(1)} %get-tuple-element.45), channel_id=1, source_target_pairs={{0,16},{8,24},{16,0},{24,8},{1,17},{9,25},{17,1},{25,9},{2,18},{10... | collective-permute-start | bytes 393224 | tf_op jit(solution)/shard_map/ppermute | solution.py:603
  24.1 7.0 %collective-permute-start.6 = (bf16[256,256]{1,0:T(8,128)(2,1)S(1)}, bf16[256,256]{1,0:T(8,128)(2,1)S(1)}, u32[]{:S(2)}, u32[]{:S(2)}) collective-permute-start(bf16[256,256]{1,0:T(8,128)(2,1)S(1)} %get-tuple-element.48.grad_ref), channel_id=1, source_target_pairs={{16,0},{24,8},{0,16},{8,24},{17,1},{25,9},{1,17},{9,25},{18,2},{26... | collective-permute-start | bytes 393224 | tf_op jit(solution)/shard_map/ppermute | solution.py:603
  28.6 6.8 %copy-start.1 = (bf16[512,16]{1,0:T(8,128)(2,1)S(1)}, bf16[512,16]{1,0:T(8,128)(2,1)}, u32[]{:S(2)}) copy-start(bf16[512,16]{1,0:T(8,128)(2,1)} %get-tuple-element.59.embedded_ref) | copy-start | bytes 49156
  28.6 6.7 %copy-start.3 = (f32[1,256]{1,0:T(1,128)S(1)}, f32[1,256]{1,0:T(1,128)}, u32[]{:S(2)}) copy-start(f32[1,256]{1,0:T(1,128)} %gain_ref.1) | copy-start | bytes 3076
  33.7 1.7 %collective-permute-start.7 = (f32[328,256]{1,0:T(8,128)S(1)}, f32[328,256]{1,0:T(8,128)S(1)}, u32[]{:S(2)}, u32[]{:S(2)}) collective-permute-start(f32[328,256]{1,0:T(8,128)S(1)} %get-tuple-element.58), channel_id=1, source_target_pairs={{0,8},{8,0},{16,24},{24,16},{1,9},{9,1},{17,25},{25,17},{2,10},{10... | collective-permute-start | bytes 1007624 | tf_op jit(solution)/shard_map/ppermute | solution.py:669

commit v3 on v2

--- a/solution.py
+++ b/solution.py
@@ -11,7 +11,7 @@
 GROUPS = 32
 EPSILON = 1e-05
 PAIR = 2
-BLOCK = 64
+BLOCK = 128
 MOD_PARTS = 4
 PREPARE_LIMIT = 60 << 20
 CHAIN_LIMIT = 48 << 20
@@ -229,12 +229,14 @@
     return stack_rows(sum_grad, sum_cross)
 
 
-def weight_products(sh, padded_ref, act_ref, slab_ref, grad_ref, sums, unit, keep_ref, send_ref, turned=False):
-    core = lax.axis_index("segment") % PAIR
-    space = lax.axis_index("space")
-    first_row = space * sh.slab
+def slab_place(sh):
+    first_row = lax.axis_index("space") * sh.slab
     first_tap = jnp.minimum(first_row // sh.channels, 9 - sh.taps)
-    offset = pl.multiple_of(first_row - first_tap * sh.channels, 8)
+    return (first_tap, pl.multiple_of(first_row - first_tap * sh.channels, 8))
+
+
+def weight_products(sh, padded_ref, act_ref, slab_ref, turned=False):
+    first_tap, _ = slab_place(sh)
     for t in range(sh.taps):
         tap = first_tap + t
         row, col = 2 - tap // 3, 2 - tap % 3
@@ -260,6 +262,11 @@
                 slab_ref[place, :] += product(i)
 
             over_chunks(sh.chunks, accumulate)
+
+
+def write_pack(sh, slab_ref, grad_ref, sums, unit, keep_ref, send_ref):
+    core = lax.axis_index("segment") % PAIR
+    _, offset = slab_place(sh)
     mine = slab_ref[pl.ds(offset, sh.slab), :]
     rows = grad_ref[own_place(sh), :]
 
@@ -445,26 +452,32 @@
         clear_edges(sh, padded_ref)
         place_upstream(sh, between_ref, padded_ref)
         for unit, above, below in ((1, laid_ref, between_ref), (0, padded_ref, grad_ref)):
-            outs = (keep_ref, send_ref)
-            weight_products(sh, above, act_ref.at[unit], slab_ref, below, sums_ref[unit], unit, *outs)
+            weight_products(sh, above, act_ref.at[unit], slab_ref)
+            write_pack(sh, slab_ref, below, sums_ref[unit], unit, keep_ref, send_ref)
 
 
 def backward_kernel(sh, active_stage, *refs):
     x_ref, middle_ref, up_ref, params_ref, weights, act_ref, slope_ref, stats_ref = refs[:8]
-    keep_ref, send_ref, grad_ref, padded_ref, pre_grad_ref, slab_ref, between_ref = refs[10:]
+    keep_ref, send_ref, grad_ref, padded_ref, pre_grad_ref, slab_ref, between_ref, second_ref, other_slab_ref = refs[10:]
     stage, _ = place_of()
 
     @pl.when(stage == active_stage)
     def _():
         clear_edges(sh, padded_ref)
-        for unit, x, above, below in ((1, middle_ref, up_ref, between_ref), (0, x_ref, between_ref, grad_ref)):
-            stats = (stats_ref[unit, 0:1, :], stats_ref[unit, 1:2, :])
-            known = (slope_ref.at[unit], stats)
+        clear_edges(sh, second_ref)
+        packs = []
+        for unit, x, above, below, shifted, slab in (
+            (1, middle_ref, up_ref, between_ref, second_ref, other_slab_ref),
+            (0, x_ref, between_ref, grad_ref, padded_ref, slab_ref),
+        ):
+            known = (slope_ref.at[unit], (stats_ref[unit, 0:1, :], stats_ref[unit, 1:2, :]))
             params = unit_params(params_ref, unit)
             own = unit == 0 and active_stage == 0
-            sums = backward_unit(sh, x, above, below, params, known, padded_ref, pre_grad_ref, weights, unit, own)
-            outs = (keep_ref, send_ref)
-            weight_products(sh, padded_ref, act_ref.at[unit], slab_ref, below, sums, unit, *outs, turned=True)
+            sums = backward_unit(sh, x, above, below, params, known, shifted, pre_grad_ref, weights, unit, own)
+            weight_products(sh, shifted, act_ref.at[unit], slab, turned=True)
+            packs.append((slab, below, sums, unit))
+        for pack in packs:
+            write_pack(sh, *pack, keep_ref, send_ref)
 
 
 def finish_kernel(sh, keep_ref, other_ref, embedded_ref, gain_ref, grads_hbm, conv_hbm, mod_hbm, *scratch):
@@ -663,7 +676,7 @@
             functools.partial(backward_kernel, sh, active),
             [VMEM] * 10,
             [pack_shape, pack_shape] + ([] if last else [image_shape]),
-            (spare if last else []) + work + slab + spare,
+            (spare if last else []) + work + slab + spare + common + slab,
             aliases={8: 0, 9: 1},
         )(entering[active], middles[active], upstream, params, turned, *noted, keep, send)
     other = lax.ppermute(send, "segment", swap)

time: 37.1 us -> 34.6 us (0.933)
  Pallas kernels: 12.2 us -> 10.9 us
  starting transfers between devices: 11.4 us -> 10.3 us
    ppermute x2, starting transfers between devices: 3.92 us -> 2.78 us  [hop(): return lax.ppermute(value, 'segment', pairs + [(b, a) for a, b in pairs])]
    pallas_call x1, Pallas kernels: 2.53 us -> 1.73 us  [shards(): call(functools.partial(backward_kernel, sh, active), [VMEM] * 10, [pack_s...]
    pallas_call x1, Pallas kernels: 2.14 us -> 1.58 us  [shards(): call(functools.partial(forward_kernel, sh, 0, (order, far_order)), [VMEM]...]
  transfers between devices with their start and end apart: 8 -> 8, of which waited for: 6 -> 6; matrix products, arithmetic and copies ran while one was open for 2% -> 2% of each run, Pallas kernels for 17% -> 18%
where the time goes in v3:
time: 34.6 us; the launch traced here: 34.2 us
  Pallas kernels  10.9 us (32%)
  waiting for transfers between devices  10.8 us (31%)
  starting transfers between devices  10.3 us (30%)
  other arithmetic  0.76 us (2%)
  between operations  0.76 us (2%)
  local copies, waits for them, and re-layouts  0.71 us (2%)
    ppermute x2, waiting for transfers between devices, hop(): return lax.ppermute(value, 'segment', pairs + [(b, a) for a, b in pairs])  7.22 us
    ppermute x3, starting transfers between devices, shards(): far = lax.ppermute(near, 'space', [(i, i ^ bit) for i in range(spaces)])  6.9 us
    ppermute x2, starting transfers between devices, hop(): return lax.ppermute(value, 'segment', pairs + [(b, a) for a, b in pairs])  2.78 us
    pallas_call x1, Pallas kernels, shards(): call(embed_kernel, [SMEM, SMEM, ANY, ANY], [shape((16, width), bf16), sha...  2.51 us
    pallas_call x1, Pallas kernels, shards(): call(modulate_kernel, [ANY] * 4, [shape((8, channels), f32)] * 2, [pltpu....  1.88 us
    pallas_call x1, Pallas kernels, shards(): call(functools.partial(backward_kernel, sh, active), [VMEM] * 10, [pack_s...  1.73 us
    ppermute x1, waiting for transfers between devices, shards(): other = lax.ppermute(send, 'segment', swap)  1.63 us
    pallas_call x1, Pallas kernels, shards(): call(functools.partial(forward_kernel, sh, 0, (order, far_order)), [VMEM]...  1.58 us
  transfers between devices with their start and end apart: 8, of which 6 were waited for; matrix products, arithmetic and copies ran while one was open for 2% of the time, Pallas kernels for 18%

profile of v3, /device:TPU:0, one launch (start us, length us, event | category | flops | bytes accessed | tf_op | source)
XLA Modules:
  0.0 34.2 jit_solution(12213007194526678699)
XLA Ops:
  0.6 0.5 %collective-permute-start.3 = (bf16[2304,256]{1,0:T(8,128)(2,1)}, bf16[2304,256]{1,0:T(8,128)(2,1)S(1)}, u32[]{:S(2)}, u32[]{:S(2)}) collective-permute-start(bf16[2304,256]{1,0:T(8,128)(2,1)} %bitcast.7), channel_id=1, source_target_pairs={{0,8},{8,0},{16,24},{24,16},{1,9},{9,1},{17,25},{25,17},{2,10},{10... | collective-permute-start | bytes 3538952 | tf_op jit(solution)/shard_map/ppermute | solution.py:559
  1.2 0.7 %dynamic-slice_select_fusion = bf16[1,2,16,256]{3,2,1,0:T(8,128)(2,1)S(1)} fusion(bf16[2,2,16,256]{3,2,1,0:T(8,128)(2,1)} %param.11, s32[]{:T(128)S(6)} %select_n.27, bf16[2,2,16,256]{3,2,1,0:T(8,128)(2,1)} %param.10, pred[]{:T(512)S(6)} %eq.5), kind=kLoop, calls=%fused_computation.2 | loop fusion | flops 8192 | bytes 49157 | tf_op jit(solution)/shard_map/jit(_where)/select_n | solution.py:560
  1.9 3.7 %collective-permute-start = (bf16[1,32,256]{2,1,0:T(8,128)(2,1)S(1)}, bf16[1,32,256]{2,1,0:T(8,128)(2,1)S(1)}, u32[]{:S(2)}, u32[]{:S(2)}) collective-permute-start(bf16[1,32,256]{2,1,0:T(8,128)(2,1)S(1)} %bitcast.11), channel_id=1, source_target_pairs={{0,4},{1,5},{2,6},{3,7},{4,0},{5,1},{6,2},{7,3},{8,12},{9,13},{10,... | collective-permute-start | bytes 49160 | tf_op jit(solution)/shard_map/ppermute | solution.py:568
  5.6 2.5 %shard_map.121 = (bf16[16,512]{1,0:T(8,128)(2,1)}, bf16[512,16]{1,0:T(8,128)(2,1)}) custom-call(s32[2]{0:T(128)} %times_ref.1, s32[2]{0:T(128)} %labels_ref.1, bf16[125,8,512]{2,1,0:T(8,128)(2,1)} %bitcast.9, bf16[128,512]{1,0:T(8,128)(2,1)} %time_weight_hbm.1), custom_call_target="tpu_custom_call" | custom-call | flops 1048576 | bytes 4194304 | tf_op jit(solution)/shard_map/pallas_call | solution.py:570
  8.1 1.6 %collective-permute-start.1 = (bf16[2,32,256]{2,1,0:T(8,128)(2,1)S(1)}, bf16[2,32,256]{2,1,0:T(8,128)(2,1)S(1)}, u32[]{:S(2)}, u32[]{:S(2)}) collective-permute-start(bf16[2,32,256]{2,1,0:T(8,128)(2,1)S(1)} %pad_maximum_fusion.1), channel_id=1, source_target_pairs={{0,2},{1,3},{2,0},{3,1},{4,6},{5,7},{6,4},{7,5},{8,10},{9,11},{10,... | collective-permute-start | bytes 98312 | tf_op jit(solution)/shard_map/ppermute | solution.py:568
  9.8 1.9 %shard_map.122 = (f32[8,256]{1,0:T(8,128)}, f32[8,256]{1,0:T(8,128)}) custom-call(bf16[16,512]{1,0:T(8,128)(2,1)} %get-tuple-element.35.embedded_hbm, bf16[512,512]{1,0:T(8,128)(2,1)} %bitcast.10, f32[1,512]{1,0:T(1,128)} %bias_hbm.1, f32[1,256]{1,0:T(1,128)} %gain_ref.1), custom_call_target="tpu_custom_call" | custom-call | flops 1048576 | bytes 4194304 | tf_op jit(solution)/shard_map/pallas_call | solution.py:586
  11.7 0.4 %collective-permute-done.1 = bf16[2,32,256]{2,1,0:T(8,128)(2,1)S(1)} collective-permute-done((bf16[2,32,256]{2,1,0:T(8,128)(2,1)S(1)}, bf16[2,32,256]{2,1,0:T(8,128)(2,1)S(1)}, u32[]{:S(2)}, u32[]{:S(2)}) %collective-permute-start.1) | collective-permute-done | bytes 32800 | tf_op jit(solution)/shard_map/ppermute | solution.py:568
  12.1 1.6 %collective-permute-start.2 = (bf16[4,32,256]{2,1,0:T(8,128)(2,1)S(1)}, bf16[4,32,256]{2,1,0:T(8,128)(2,1)S(1)}, u32[]{:S(2)}, u32[]{:S(2)}) collective-permute-start(bf16[4,32,256]{2,1,0:T(8,128)(2,1)S(1)} %pad_maximum_fusion.refs_0_), channel_id=1, source_target_pairs={{0,1},{1,0},{2,3},{3,2},{4,5},{5,4},{6,7},{7,6},{8,9},{9,8},{10,11... | collective-permute-start | bytes 196616 | tf_op jit(solution)/shard_map/ppermute | solution.py:568
  13.7 1.4 %collective-permute-done.4.mod_other_any = f32[8,256]{1,0:T(8,128)S(1)} collective-permute-done((f32[8,256]{1,0:T(8,128)}, f32[8,256]{1,0:T(8,128)S(1)}, u32[]{:S(2)}, u32[]{:S(2)}) %collective-permute-start.4) | collective-permute-done | bytes 8224 | tf_op jit(solution)/shard_map/ppermute | solution.py:601
  15.1 0.7 %copy-done.2 = f32[8,256]{1,0:T(8,128)S(1)} copy-done((f32[8,256]{1,0:T(8,128)S(1)}, f32[8,256]{1,0:T(8,128)}, u32[]{:S(2)}) %copy-start.2) | copy-done | bytes 8216
  15.8 0.5 %shard_map.123 = (bf16[2,2304,256]{2,1,0:T(8,128)(2,1)S(1)}, f32[8,256]{1,0:T(8,128)S(1)}) custom-call(bf16[2304,256]{1,0:T(8,128)(2,1)S(1)} %bitcast.8, bf16[2304,256]{1,0:T(8,128)(2,1)S(1)} %collective-permute-done.3.other_any, f32[8,256]{1,0:T(8,128)S(1)} %copy-done.2, f32[8,256]{1,0:T(8,128)S(1)} %collective-permute-done.4.mod_other_any), custom_call_target="tpu_custom_call" | custom-call | flops 1048576 | bytes 4194304 | tf_op jit(solution)/shard_map/pallas_call | solution.py:602
  16.3 0.2 collective-permute-done.2.refs_1_
  16.5 1.6 %shard_map.124 = (bf16[256,256]{1,0:T(8,128)(2,1)S(1)}, bf16[256,256]{1,0:T(8,128)(2,1)S(1)}, bf16[256,256]{1,0:T(8,128)(2,1)S(1)}) custom-call(bf16[4,32,256]{2,1,0:T(8,128)(2,1)S(1)} %pad_maximum_fusion.refs_0_, bf16[4,32,256]{2,1,0:T(8,128)(2,1)S(1)} %collective-permute-done.2.refs_1_, f32[8,256]{1,0:T(8,128)S(1)} %get-tuple-element.41.refs_2_.params_ref.refs_3_, ...), custom_call_target="tpu_custom_call" | custom-call | tf_op jit(solution)/shard_map/pallas_call | solution.py:618
  18.1 0.1 collective-permute-start.5
  18.1 0.7 %shard_map.125 = (bf16[3,288,256]{2,1,0:T(8,128)(2,1)S(1)}, bf16[2,2304,256]{2,1,0:T(8,128)(2,1)S(1)}) custom-call(bf16[256,256]{1,0:T(8,128)(2,1)S(1)} %get-tuple-element.43.up_ref.x_ref.refs_0_, bf16[2,2304,256]{2,1,0:T(8,128)(2,1)S(1)} %get-tuple-element.42.refs_3_.weights_ref.weights), custom_call_target="tpu_custom_call" | custom-call | flops 1048576 | bytes 4194304 | tf_op jit(solution)/shard_map/pallas_call | solution.py:652
  18.8 4.7 %collective-permute-done.5.x_ref = bf16[256,256]{1,0:T(8,128)(2,1)S(1)} collective-permute-done((bf16[256,256]{1,0:T(8,128)(2,1)S(1)}, bf16[256,256]{1,0:T(8,128)(2,1)S(1)}, u32[]{:S(2)}, u32[]{:S(2)}) %collective-permute-start.5) | collective-permute-done | bytes 131104 | tf_op jit(solution)/shard_map/ppermute | solution.py:616
  23.6 2.7 %collective-permute-start.6 = (bf16[256,256]{1,0:T(8,128)(2,1)S(1)}, bf16[256,256]{1,0:T(8,128)(2,1)S(1)}, u32[]{:S(2)}, u32[]{:S(2)}) collective-permute-start(bf16[256,256]{1,0:T(8,128)(2,1)S(1)} %get-tuple-element.48.grad_ref), channel_id=1, source_target_pairs={{16,0},{24,8},{0,16},{8,24},{17,1},{25,9},{1,17},{9,25},{18,2},{26... | collective-permute-start | bytes 393224 | tf_op jit(solution)/shard_map/ppermute | solution.py:616
  26.3 0.6 %shard_map.127 = (bf16[2,256,256]{2,1,0:T(8,128)(2,1)S(1)}, f32[2,256,256]{2,1,0:T(8,128)S(1)}, f32[2,8,256]{2,1,0:T(8,128)S(1)}) custom-call(bf16[256,256]{1,0:T(8,128)(2,1)S(1)} %get-tuple-element.43.up_ref.x_ref.refs_0_, bf16[256,256]{1,0:T(8,128)(2,1)S(1)} %get-tuple-element.44.middle_ref.refs_1_, f32[8,256]{1,0:T(8,128)S(1)} %get-tuple-element.41.refs_2_.params_ref.refs_3_), custom_call_target="tpu_custom_call" | custom-call | flops 1048576 | bytes 4194304 | tf_op jit(solution)/shard_map/pallas_call | solution.py:637
  26.9 0.0 copy-start.1
  27.0 2.5 %collective-permute-done.6.refs_2_ = bf16[256,256]{1,0:T(8,128)(2,1)S(1)} collective-permute-done((bf16[256,256]{1,0:T(8,128)(2,1)S(1)}, bf16[256,256]{1,0:T(8,128)(2,1)S(1)}, u32[]{:S(2)}, u32[]{:S(2)}) %collective-permute-start.6) | collective-permute-done | bytes 131104 | tf_op jit(solution)/shard_map/ppermute | solution.py:616
  29.4 1.7 %shard_map.129 = (f32[328,256]{1,0:T(8,128)S(1)}, f32[328,256]{1,0:T(8,128)S(1)}) custom-call(bf16[256,256]{1,0:T(8,128)(2,1)S(1)} %get-tuple-element.43.up_ref.x_ref.refs_0_, bf16[256,256]{1,0:T(8,128)(2,1)S(1)} %get-tuple-element.44.middle_ref.refs_1_, ...), custom_call_target="tpu_custom_call", output_to_operand_aliasing={{0}: (8, {}), {1}: (9, {})} | custom-call | tf_op jit(solution)/shard_map/pallas_call | solution.py:675
  31.2 0.1 collective-permute-start.7
  31.3 1.6 %collective-permute-done.7.other_ref = f32[328,256]{1,0:T(8,128)S(1)} collective-permute-done((f32[328,256]{1,0:T(8,128)S(1)}, f32[328,256]{1,0:T(8,128)S(1)}, u32[]{:S(2)}, u32[]{:S(2)}) %collective-permute-start.7) | collective-permute-done | bytes 335904 | tf_op jit(solution)/shard_map/ppermute | solution.py:682
  32.9 1.3 %shard_map.130 = (bf16[2,32,256]{2,1,0:T(8,128)(2,1)}, f32[288,256]{1,0:T(8,128)}, f32[512,512]{1,0:T(8,128)}) custom-call(f32[328,256]{1,0:T(8,128)S(1)} %get-tuple-element.57.keep_ref, f32[328,256]{1,0:T(8,128)S(1)} %collective-permute-done.7.other_ref, bf16[512,16]{1,0:T(8,128)(2,1)S(1)} %copy-done.1, f32[1,256]{1,0:T(1,128)S(1)} %copy-done.3), custom_call_target="tpu_custom_call" | custom-call | tf_op jit(solution)/shard_map/pallas_call | solution.py:688
  (13 shorter events, 0.1 us)
Async XLA Ops:
  0.6 14.5 %copy-start = (bf16[1,3,3,256,256]{4,3,2,1,0:T(8,128)(2,1)S(1)}, bf16[1,3,3,256,256]{4,3,2,1,0:T(8,128)(2,1)}, u32[]{:S(2)}) copy-start(bf16[1,3,3,256,256]{4,3,2,1,0:T(8,128)(2,1)} %param.16) | copy-start | bytes 3538948
  0.6 14.4 %collective-permute-start.3 = (bf16[2304,256]{1,0:T(8,128)(2,1)}, bf16[2304,256]{1,0:T(8,128)(2,1)S(1)}, u32[]{:S(2)}, u32[]{:S(2)}) collective-permute-start(bf16[2304,256]{1,0:T(8,128)(2,1)} %bitcast.7), channel_id=1, source_target_pairs={{0,8},{8,0},{16,24},{24,16},{1,9},{9,1},{17,25},{25,17},{2,10},{10... | collective-permute-start | bytes 3538952 | tf_op jit(solution)/shard_map/ppermute | solution.py:559
  1.9 6.2 %collective-permute-start = (bf16[1,32,256]{2,1,0:T(8,128)(2,1)S(1)}, bf16[1,32,256]{2,1,0:T(8,128)(2,1)S(1)}, u32[]{:S(2)}, u32[]{:S(2)}) collective-permute-start(bf16[1,32,256]{2,1,0:T(8,128)(2,1)S(1)} %bitcast.11), channel_id=1, source_target_pairs={{0,4},{1,5},{2,6},{3,7},{4,0},{5,1},{6,2},{7,3},{8,12},{9,13},{10,... | collective-permute-start | bytes 49160 | tf_op jit(solution)/shard_map/ppermute | solution.py:568
  8.1 4.0 %collective-permute-start.1 = (bf16[2,32,256]{2,1,0:T(8,128)(2,1)S(1)}, bf16[2,32,256]{2,1,0:T(8,128)(2,1)S(1)}, u32[]{:S(2)}, u32[]{:S(2)}) collective-permute-start(bf16[2,32,256]{2,1,0:T(8,128)(2,1)S(1)} %pad_maximum_fusion.1), channel_id=1, source_target_pairs={{0,2},{1,3},{2,0},{3,1},{4,6},{5,7},{6,4},{7,5},{8,10},{9,11},{10,... | collective-permute-start | bytes 98312 | tf_op jit(solution)/shard_map/ppermute | solution.py:568
  12.1 4.3 %collective-permute-start.2 = (bf16[4,32,256]{2,1,0:T(8,128)(2,1)S(1)}, bf16[4,32,256]{2,1,0:T(8,128)(2,1)S(1)}, u32[]{:S(2)}, u32[]{:S(2)}) collective-permute-start(bf16[4,32,256]{2,1,0:T(8,128)(2,1)S(1)} %pad_maximum_fusion.refs_0_), channel_id=1, source_target_pairs={{0,1},{1,0},{2,3},{3,2},{4,5},{5,4},{6,7},{7,6},{8,9},{9,8},{10,11... | collective-permute-start | bytes 196616 | tf_op jit(solution)/shard_map/ppermute | solution.py:568
  13.7 1.4 %collective-permute-start.4 = (f32[8,256]{1,0:T(8,128)}, f32[8,256]{1,0:T(8,128)S(1)}, u32[]{:S(2)}, u32[]{:S(2)}) collective-permute-start(f32[8,256]{1,0:T(8,128)} %get-tuple-element.40), channel_id=1, source_target_pairs={{0,8},{8,0},{16,24},{24,16},{1,9},{9,1},{17,25},{25,17},{2,10},{10... | collective-permute-start | bytes 24584 | tf_op jit(solution)/shard_map/ppermute | solution.py:601
  15.1 0.7 %copy-start.2 = (f32[8,256]{1,0:T(8,128)S(1)}, f32[8,256]{1,0:T(8,128)}, u32[]{:S(2)}) copy-start(f32[8,256]{1,0:T(8,128)} %get-tuple-element.39.mod_keep_any) | copy-start | bytes 24580
  18.1 5.5 %collective-permute-start.5 = (bf16[256,256]{1,0:T(8,128)(2,1)S(1)}, bf16[256,256]{1,0:T(8,128)(2,1)S(1)}, u32[]{:S(2)}, u32[]{:S(2)}) collective-permute-start(bf16[256,256]{1,0:T(8,128)(2,1)S(1)} %get-tuple-element.45), channel_id=1, source_target_pairs={{0,16},{8,24},{16,0},{24,8},{1,17},{9,25},{17,1},{25,9},{2,18},{10... | collective-permute-start | bytes 393224 | tf_op jit(solution)/shard_map/ppermute | solution.py:616
  23.6 5.9 %collective-permute-start.6 = (bf16[256,256]{1,0:T(8,128)(2,1)S(1)}, bf16[256,256]{1,0:T(8,128)(2,1)S(1)}, u32[]{:S(2)}, u32[]{:S(2)}) collective-permute-start(bf16[256,256]{1,0:T(8,128)(2,1)S(1)} %get-tuple-element.48.grad_ref), channel_id=1, source_target_pairs={{16,0},{24,8},{0,16},{8,24},{17,1},{25,9},{1,17},{9,25},{18,2},{26... | collective-permute-start | bytes 393224 | tf_op jit(solution)/shard_map/ppermute | solution.py:616
  26.9 6.0 %copy-start.1 = (bf16[512,16]{1,0:T(8,128)(2,1)S(1)}, bf16[512,16]{1,0:T(8,128)(2,1)}, u32[]{:S(2)}) copy-start(bf16[512,16]{1,0:T(8,128)(2,1)} %get-tuple-element.59.embedded_ref) | copy-start | bytes 49156
  26.9 5.9 %copy-start.3 = (f32[1,256]{1,0:T(1,128)S(1)}, f32[1,256]{1,0:T(1,128)}, u32[]{:S(2)}) copy-start(f32[1,256]{1,0:T(1,128)} %gain_ref.1) | copy-start | bytes 3076
  31.2 1.7 %collective-permute-start.7 = (f32[328,256]{1,0:T(8,128)S(1)}, f32[328,256]{1,0:T(8,128)S(1)}, u32[]{:S(2)}, u32[]{:S(2)}) collective-permute-start(f32[328,256]{1,0:T(8,128)S(1)} %get-tuple-element.58), channel_id=1, source_target_pairs={{0,8},{8,0},{16,24},{24,16},{1,9},{9,1},{17,25},{25,17},{2,10},{10... | collective-permute-start | bytes 1007624 | tf_op jit(solution)/shard_map/ppermute | solution.py:682

commit v4 on v1

--- a/solution.py
+++ b/solution.py
@@ -114,26 +114,17 @@
     ).astype(jnp.bfloat16)
 
 
-def convolve(sh, padded_ref, start, weight_ref, unit, backward):
-    size = min(BLOCK, sh.chunk)
-    totals = []
-    for first in range(0, sh.chunk, size):
-        total = None
-        for p in range(3):
-            for q in range(3):
-                row, col = (2 - p, 2 - q) if backward else (p, q)
-                block = padded_ref[col, pl.ds(start + first + row * sh.cols, size), :]
-                tap = (3 * p + q) * sh.channels
-                weight = weight_ref[unit, tap : tap + sh.channels, :]
-                part = lax.dot_general(
-                    block,
-                    weight,
-                    (((1,), (0,)), ((), ())),
-                    preferred_element_type=jnp.float32,
-                )
-                total = part if total is None else total + part
-        totals.append(total)
-    return totals[0] if len(totals) == 1 else jnp.concatenate(totals, axis=0)
+def convolve(sh, padded_ref, start, size, weight_ref, unit, backward):
+    total = None
+    for p in range(3):
+        for q in range(3):
+            row, col = (2 - p, 2 - q) if backward else (p, q)
+            block = padded_ref[col, pl.ds(start + row * sh.cols, size), :]
+            tap = (3 * p + q) * sh.channels
+            weight = weight_ref[unit, tap : tap + sh.channels, :]
+            part = jnp.dot(block, weight, preferred_element_type=jnp.float32)
+            total = part if total is None else total + part
+    return total
 
 
 def activation(sh, x_ref, place, stats, params):
@@ -172,10 +163,12 @@
             slope_ref[place, :] = slope
 
     def produce(i):
-        start = chunk_start(i, sh.chunk)
-        inputs = x_ref[pl.ds(start, sh.chunk), :].astype(jnp.float32)
-        z = convolve(sh, padded_ref, start, weight_ref, unit, False)
-        out_ref[pl.ds(start, sh.chunk), :] = (inputs + z).astype(jnp.bfloat16)
+        size = min(BLOCK, sh.chunk)
+        for first in range(0, sh.chunk, size):
+            start = chunk_start(i, sh.chunk) + first
+            inputs = x_ref[pl.ds(start, size), :].astype(jnp.float32)
+            z = convolve(sh, padded_ref, start, size, weight_ref, unit, False)
+            out_ref[pl.ds(start, size), :] = (inputs + z).astype(jnp.bfloat16)
 
     over_chunks(sh.chunks, activate)
     over_chunks(sh.chunks, produce)
@@ -200,12 +193,15 @@
     zero = jnp.zeros((8, sh.channels), jnp.float32)
 
     def differentiate(i, sums):
-        start = chunk_start(i, sh.chunk)
-        rows = pl.ds(start, sh.chunk)
-        normed = (x_ref[rows, :].astype(jnp.float32) - mean) * inv_std
-        pre_grad = convolve(sh, padded_ref, start, weight_ref, unit, True) * slope_ref[rows, :]
-        pre_grad_ref[rows, :] = pre_grad
-        return (sums[0] + fold_rows(pre_grad), sums[1] + fold_rows(pre_grad * normed))
+        size = min(BLOCK, sh.chunk)
+        for first in range(0, sh.chunk, size):
+            start = chunk_start(i, sh.chunk) + first
+            rows = pl.ds(start, size)
+            normed = (x_ref[rows, :].astype(jnp.float32) - mean) * inv_std
+            pre_grad = convolve(sh, padded_ref, start, size, weight_ref, unit, True) * slope_ref[rows, :]
+            pre_grad_ref[rows, :] = pre_grad
+            sums = (sums[0] + fold_rows(pre_grad), sums[1] + fold_rows(pre_grad * normed))
+        return sums
 
     if not placed:
         place_upstream(sh, up_ref, padded_ref)

time: 34.5 us -> 34.4 us (level)
  no operation moved by 1% of the time
where the time goes in v4:
time: 34.4 us; the launch traced here: 34 us
  waiting for transfers between devices  10.8 us (31%)
  Pallas kernels  10.7 us (31%)
  starting transfers between devices  10.3 us (30%)
  other arithmetic  0.76 us (2%)
  between operations  0.76 us (2%)
  local copies, waits for them, and re-layouts  0.71 us (2%)
    ppermute x2, waiting for transfers between devices, hop(): return lax.ppermute(value, 'segment', pairs + [(b, a) for a, b in pairs])  7.22 us
    ppermute x3, starting transfers between devices, shards(): far = lax.ppermute(near, 'space', [(i, i ^ bit) for i in range(spaces)])  6.9 us
    ppermute x2, starting transfers between devices, hop(): return lax.ppermute(value, 'segment', pairs + [(b, a) for a, b in pairs])  2.78 us
    pallas_call x1, Pallas kernels, shards(): call(embed_kernel, [SMEM, SMEM, ANY, ANY], [shape((16, width), bf16)], [p...  2.36 us
    pallas_call x1, Pallas kernels, shards(): call(modulate_kernel, [ANY] * 4, [shape((8, channels), f32)] * 2, [pltpu....  1.88 us
    pallas_call x1, Pallas kernels, shards(): call(functools.partial(backward_kernel, sh, active), [VMEM] * 10, [pack_s...  1.67 us
    ppermute x1, waiting for transfers between devices, shards(): other = lax.ppermute(send, 'segment', swap)  1.63 us
    pallas_call x1, Pallas kernels, shards(): call(functools.partial(forward_kernel, sh, 0, (order, far_order)), [VMEM]...  1.58 us
  transfers between devices with their start and end apart: 8, of which 6 were waited for; matrix products, arithmetic and copies ran while one was open for 2% of the time, Pallas kernels for 18%

profile of v4, /device:TPU:0, one launch (start us, length us, event | category | flops | bytes accessed | tf_op | source)
XLA Modules:
  0.0 34.0 jit_solution(7109798004572809411)
XLA Ops:
  0.6 0.5 %collective-permute-start.3 = (bf16[2304,256]{1,0:T(8,128)(2,1)}, bf16[2304,256]{1,0:T(8,128)(2,1)S(1)}, u32[]{:S(2)}, u32[]{:S(2)}) collective-permute-start(bf16[2304,256]{1,0:T(8,128)(2,1)} %bitcast.7), channel_id=1, source_target_pairs={{0,8},{8,0},{16,24},{24,16},{1,9},{9,1},{17,25},{25,17},{2,10},{10... | collective-permute-start | bytes 3538952 | tf_op jit(solution)/shard_map/ppermute | solution.py:539
  1.2 0.7 %dynamic-slice_select_fusion = bf16[1,2,16,256]{3,2,1,0:T(8,128)(2,1)S(1)} fusion(bf16[2,2,16,256]{3,2,1,0:T(8,128)(2,1)} %param.11, s32[]{:T(128)S(6)} %select_n.27, bf16[2,2,16,256]{3,2,1,0:T(8,128)(2,1)} %param.10, pred[]{:T(512)S(6)} %eq.5), kind=kLoop, calls=%fused_computation.2 | loop fusion | flops 8192 | bytes 49157 | tf_op jit(solution)/shard_map/jit(_where)/select_n | solution.py:540
  1.9 3.7 %collective-permute-start = (bf16[1,32,256]{2,1,0:T(8,128)(2,1)S(1)}, bf16[1,32,256]{2,1,0:T(8,128)(2,1)S(1)}, u32[]{:S(2)}, u32[]{:S(2)}) collective-permute-start(bf16[1,32,256]{2,1,0:T(8,128)(2,1)S(1)} %bitcast.11), channel_id=1, source_target_pairs={{0,4},{1,5},{2,6},{3,7},{4,0},{5,1},{6,2},{7,3},{8,12},{9,13},{10,... | collective-permute-start | bytes 49160 | tf_op jit(solution)/shard_map/ppermute | solution.py:548
  5.6 2.4 %shard_map.121.embedded_hbm.embedded_ref = bf16[16,512]{1,0:T(8,128)(2,1)} custom-call(s32[2]{0:T(128)} %times_ref.1, s32[2]{0:T(128)} %labels_ref.1, bf16[125,8,512]{2,1,0:T(8,128)(2,1)} %bitcast.9, bf16[128,512]{1,0:T(8,128)(2,1)} %time_weight_hbm.1), custom_call_target="tpu_custom_call" | custom-call | flops 1048576 | bytes 4194304 | tf_op jit(solution)/shard_map/pallas_call | solution.py:550
  8.0 1.6 %collective-permute-start.1 = (bf16[2,32,256]{2,1,0:T(8,128)(2,1)S(1)}, bf16[2,32,256]{2,1,0:T(8,128)(2,1)S(1)}, u32[]{:S(2)}, u32[]{:S(2)}) collective-permute-start(bf16[2,32,256]{2,1,0:T(8,128)(2,1)S(1)} %pad_maximum_fusion.1), channel_id=1, source_target_pairs={{0,2},{1,3},{2,0},{3,1},{4,6},{5,7},{6,4},{7,5},{8,10},{9,11},{10,... | collective-permute-start | bytes 98312 | tf_op jit(solution)/shard_map/ppermute | solution.py:548
  9.6 1.9 %shard_map.122 = (f32[8,256]{1,0:T(8,128)}, f32[8,256]{1,0:T(8,128)}) custom-call(bf16[16,512]{1,0:T(8,128)(2,1)} %shard_map.121.embedded_hbm.embedded_ref, bf16[512,512]{1,0:T(8,128)(2,1)} %bitcast.10, f32[1,512]{1,0:T(1,128)} %bias_hbm.1, f32[1,256]{1,0:T(1,128)} %gain_ref.1), custom_call_target="tpu_custom_call" | custom-call | flops 1048576 | bytes 4194304 | tf_op jit(solution)/shard_map/pallas_call | solution.py:566
  11.5 0.4 %collective-permute-done.1 = bf16[2,32,256]{2,1,0:T(8,128)(2,1)S(1)} collective-permute-done((bf16[2,32,256]{2,1,0:T(8,128)(2,1)S(1)}, bf16[2,32,256]{2,1,0:T(8,128)(2,1)S(1)}, u32[]{:S(2)}, u32[]{:S(2)}) %collective-permute-start.1) | collective-permute-done | bytes 32800 | tf_op jit(solution)/shard_map/ppermute | solution.py:548
  12.0 1.6 %collective-permute-start.2 = (bf16[4,32,256]{2,1,0:T(8,128)(2,1)S(1)}, bf16[4,32,256]{2,1,0:T(8,128)(2,1)S(1)}, u32[]{:S(2)}, u32[]{:S(2)}) collective-permute-start(bf16[4,32,256]{2,1,0:T(8,128)(2,1)S(1)} %pad_maximum_fusion.refs_0_), channel_id=1, source_target_pairs={{0,1},{1,0},{2,3},{3,2},{4,5},{5,4},{6,7},{7,6},{8,9},{9,8},{10,11... | collective-permute-start | bytes 196616 | tf_op jit(solution)/shard_map/ppermute | solution.py:548
  13.5 1.4 %collective-permute-done.4.mod_other_any = f32[8,256]{1,0:T(8,128)S(1)} collective-permute-done((f32[8,256]{1,0:T(8,128)}, f32[8,256]{1,0:T(8,128)S(1)}, u32[]{:S(2)}, u32[]{:S(2)}) %collective-permute-start.4) | collective-permute-done | bytes 8224 | tf_op jit(solution)/shard_map/ppermute | solution.py:581
  14.9 0.7 %copy-done.2 = f32[8,256]{1,0:T(8,128)S(1)} copy-done((f32[8,256]{1,0:T(8,128)S(1)}, f32[8,256]{1,0:T(8,128)}, u32[]{:S(2)}) %copy-start.2) | copy-done | bytes 8216
  15.6 0.5 %shard_map.123 = (bf16[2,2304,256]{2,1,0:T(8,128)(2,1)S(1)}, f32[8,256]{1,0:T(8,128)S(1)}) custom-call(bf16[2304,256]{1,0:T(8,128)(2,1)S(1)} %bitcast.8, bf16[2304,256]{1,0:T(8,128)(2,1)S(1)} %collective-permute-done.3.other_any, f32[8,256]{1,0:T(8,128)S(1)} %copy-done.2, f32[8,256]{1,0:T(8,128)S(1)} %collective-permute-done.4.mod_other_any), custom_call_target="tpu_custom_call" | custom-call | flops 1048576 | bytes 4194304 | tf_op jit(solution)/shard_map/pallas_call | solution.py:582
  16.2 0.2 collective-permute-done.2.refs_1_
  16.3 1.6 %shard_map.124 = (bf16[256,256]{1,0:T(8,128)(2,1)S(1)}, bf16[256,256]{1,0:T(8,128)(2,1)S(1)}, bf16[256,256]{1,0:T(8,128)(2,1)S(1)}) custom-call(bf16[4,32,256]{2,1,0:T(8,128)(2,1)S(1)} %pad_maximum_fusion.refs_0_, bf16[4,32,256]{2,1,0:T(8,128)(2,1)S(1)} %collective-permute-done.2.refs_1_, f32[8,256]{1,0:T(8,128)S(1)} %get-tuple-element.38.refs_2_.params_ref.refs_3_, ...), custom_call_target="tpu_custom_call" | custom-call | tf_op jit(solution)/shard_map/pallas_call | solution.py:598
  17.9 0.1 collective-permute-start.5
  18.0 0.7 %shard_map.125 = (bf16[3,288,256]{2,1,0:T(8,128)(2,1)S(1)}, bf16[2,2304,256]{2,1,0:T(8,128)(2,1)S(1)}) custom-call(bf16[256,256]{1,0:T(8,128)(2,1)S(1)} %get-tuple-element.40.up_ref.x_ref.refs_0_, bf16[2,2304,256]{2,1,0:T(8,128)(2,1)S(1)} %get-tuple-element.39.refs_3_.weights_ref.weights), custom_call_target="tpu_custom_call" | custom-call | flops 1048576 | bytes 4194304 | tf_op jit(solution)/shard_map/pallas_call | solution.py:632
  18.7 4.7 %collective-permute-done.5.x_ref = bf16[256,256]{1,0:T(8,128)(2,1)S(1)} collective-permute-done((bf16[256,256]{1,0:T(8,128)(2,1)S(1)}, bf16[256,256]{1,0:T(8,128)(2,1)S(1)}, u32[]{:S(2)}, u32[]{:S(2)}) %collective-permute-start.5) | collective-permute-done | bytes 131104 | tf_op jit(solution)/shard_map/ppermute | solution.py:596
  23.4 2.7 %collective-permute-start.6 = (bf16[256,256]{1,0:T(8,128)(2,1)S(1)}, bf16[256,256]{1,0:T(8,128)(2,1)S(1)}, u32[]{:S(2)}, u32[]{:S(2)}) collective-permute-start(bf16[256,256]{1,0:T(8,128)(2,1)S(1)} %get-tuple-element.45.grad_ref), channel_id=1, source_target_pairs={{16,0},{24,8},{0,16},{8,24},{17,1},{25,9},{1,17},{9,25},{18,2},{26... | collective-permute-start | bytes 393224 | tf_op jit(solution)/shard_map/ppermute | solution.py:596
  26.1 0.6 %shard_map.127 = (bf16[2,256,256]{2,1,0:T(8,128)(2,1)S(1)}, f32[2,256,256]{2,1,0:T(8,128)S(1)}, f32[2,8,256]{2,1,0:T(8,128)S(1)}) custom-call(bf16[256,256]{1,0:T(8,128)(2,1)S(1)} %get-tuple-element.40.up_ref.x_ref.refs_0_, bf16[256,256]{1,0:T(8,128)(2,1)S(1)} %get-tuple-element.41.middle_ref.refs_1_, f32[8,256]{1,0:T(8,128)S(1)} %get-tuple-element.38.refs_2_.params_ref.refs_3_), custom_call_target="tpu_custom_call" | custom-call | flops 1048576 | bytes 4194304 | tf_op jit(solution)/shard_map/pallas_call | solution.py:617
  26.8 0.0 copy-start.1
  26.8 2.5 %collective-permute-done.6.refs_2_ = bf16[256,256]{1,0:T(8,128)(2,1)S(1)} collective-permute-done((bf16[256,256]{1,0:T(8,128)(2,1)S(1)}, bf16[256,256]{1,0:T(8,128)(2,1)S(1)}, u32[]{:S(2)}, u32[]{:S(2)}) %collective-permute-start.6) | collective-permute-done | bytes 131104 | tf_op jit(solution)/shard_map/ppermute | solution.py:596
  29.3 1.7 %shard_map.129 = (f32[328,256]{1,0:T(8,128)S(1)}, f32[328,256]{1,0:T(8,128)S(1)}) custom-call(bf16[256,256]{1,0:T(8,128)(2,1)S(1)} %get-tuple-element.40.up_ref.x_ref.refs_0_, bf16[256,256]{1,0:T(8,128)(2,1)S(1)} %get-tuple-element.41.middle_ref.refs_1_, ...), custom_call_target="tpu_custom_call", output_to_operand_aliasing={{0}: (8, {}), {1}: (9, {})} | custom-call | tf_op jit(solution)/shard_map/pallas_call | solution.py:655
  31.0 0.1 collective-permute-start.7
  31.1 1.6 %collective-permute-done.7.other_ref = f32[328,256]{1,0:T(8,128)S(1)} collective-permute-done((f32[328,256]{1,0:T(8,128)S(1)}, f32[328,256]{1,0:T(8,128)S(1)}, u32[]{:S(2)}, u32[]{:S(2)}) %collective-permute-start.7) | collective-permute-done | bytes 335904 | tf_op jit(solution)/shard_map/ppermute | solution.py:662
  32.7 1.3 %shard_map.130 = (bf16[2,32,256]{2,1,0:T(8,128)(2,1)}, f32[288,256]{1,0:T(8,128)}, f32[512,512]{1,0:T(8,128)}) custom-call(f32[328,256]{1,0:T(8,128)S(1)} %get-tuple-element.54.keep_ref, f32[328,256]{1,0:T(8,128)S(1)} %collective-permute-done.7.other_ref, bf16[16,512]{1,0:T(8,128)(2,1)S(1)} %copy-done.1, f32[1,256]{1,0:T(1,128)S(1)} %copy-done.3), custom_call_target="tpu_custom_call" | custom-call | tf_op jit(solution)/shard_map/pallas_call | solution.py:668
  (13 shorter events, 0.1 us)
Async XLA Ops:
  0.6 14.3 %copy-start = (bf16[1,3,3,256,256]{4,3,2,1,0:T(8,128)(2,1)S(1)}, bf16[1,3,3,256,256]{4,3,2,1,0:T(8,128)(2,1)}, u32[]{:S(2)}) copy-start(bf16[1,3,3,256,256]{4,3,2,1,0:T(8,128)(2,1)} %param.16) | copy-start | bytes 3538948
  0.6 14.3 %collective-permute-start.3 = (bf16[2304,256]{1,0:T(8,128)(2,1)}, bf16[2304,256]{1,0:T(8,128)(2,1)S(1)}, u32[]{:S(2)}, u32[]{:S(2)}) collective-permute-start(bf16[2304,256]{1,0:T(8,128)(2,1)} %bitcast.7), channel_id=1, source_target_pairs={{0,8},{8,0},{16,24},{24,16},{1,9},{9,1},{17,25},{25,17},{2,10},{10... | collective-permute-start | bytes 3538952 | tf_op jit(solution)/shard_map/ppermute | solution.py:539
  1.9 6.1 %collective-permute-start = (bf16[1,32,256]{2,1,0:T(8,128)(2,1)S(1)}, bf16[1,32,256]{2,1,0:T(8,128)(2,1)S(1)}, u32[]{:S(2)}, u32[]{:S(2)}) collective-permute-start(bf16[1,32,256]{2,1,0:T(8,128)(2,1)S(1)} %bitcast.11), channel_id=1, source_target_pairs={{0,4},{1,5},{2,6},{3,7},{4,0},{5,1},{6,2},{7,3},{8,12},{9,13},{10,... | collective-permute-start | bytes 49160 | tf_op jit(solution)/shard_map/ppermute | solution.py:548
  8.0 4.0 %collective-permute-start.1 = (bf16[2,32,256]{2,1,0:T(8,128)(2,1)S(1)}, bf16[2,32,256]{2,1,0:T(8,128)(2,1)S(1)}, u32[]{:S(2)}, u32[]{:S(2)}) collective-permute-start(bf16[2,32,256]{2,1,0:T(8,128)(2,1)S(1)} %pad_maximum_fusion.1), channel_id=1, source_target_pairs={{0,2},{1,3},{2,0},{3,1},{4,6},{5,7},{6,4},{7,5},{8,10},{9,11},{10,... | collective-permute-start | bytes 98312 | tf_op jit(solution)/shard_map/ppermute | solution.py:548
  12.0 4.3 %collective-permute-start.2 = (bf16[4,32,256]{2,1,0:T(8,128)(2,1)S(1)}, bf16[4,32,256]{2,1,0:T(8,128)(2,1)S(1)}, u32[]{:S(2)}, u32[]{:S(2)}) collective-permute-start(bf16[4,32,256]{2,1,0:T(8,128)(2,1)S(1)} %pad_maximum_fusion.refs_0_), channel_id=1, source_target_pairs={{0,1},{1,0},{2,3},{3,2},{4,5},{5,4},{6,7},{7,6},{8,9},{9,8},{10,11... | collective-permute-start | bytes 196616 | tf_op jit(solution)/shard_map/ppermute | solution.py:548
  13.5 1.4 %collective-permute-start.4 = (f32[8,256]{1,0:T(8,128)}, f32[8,256]{1,0:T(8,128)S(1)}, u32[]{:S(2)}, u32[]{:S(2)}) collective-permute-start(f32[8,256]{1,0:T(8,128)} %get-tuple-element.37), channel_id=1, source_target_pairs={{0,8},{8,0},{16,24},{24,16},{1,9},{9,1},{17,25},{25,17},{2,10},{10... | collective-permute-start | bytes 24584 | tf_op jit(solution)/shard_map/ppermute | solution.py:581
  14.9 0.7 %copy-start.2 = (f32[8,256]{1,0:T(8,128)S(1)}, f32[8,256]{1,0:T(8,128)}, u32[]{:S(2)}) copy-start(f32[8,256]{1,0:T(8,128)} %get-tuple-element.36.mod_keep_any) | copy-start | bytes 24580
  17.9 5.5 %collective-permute-start.5 = (bf16[256,256]{1,0:T(8,128)(2,1)S(1)}, bf16[256,256]{1,0:T(8,128)(2,1)S(1)}, u32[]{:S(2)}, u32[]{:S(2)}) collective-permute-start(bf16[256,256]{1,0:T(8,128)(2,1)S(1)} %get-tuple-element.42), channel_id=1, source_target_pairs={{0,16},{8,24},{16,0},{24,8},{1,17},{9,25},{17,1},{25,9},{2,18},{10... | collective-permute-start | bytes 393224 | tf_op jit(solution)/shard_map/ppermute | solution.py:596
  23.4 5.9 %collective-permute-start.6 = (bf16[256,256]{1,0:T(8,128)(2,1)S(1)}, bf16[256,256]{1,0:T(8,128)(2,1)S(1)}, u32[]{:S(2)}, u32[]{:S(2)}) collective-permute-start(bf16[256,256]{1,0:T(8,128)(2,1)S(1)} %get-tuple-element.45.grad_ref), channel_id=1, source_target_pairs={{16,0},{24,8},{0,16},{8,24},{17,1},{25,9},{1,17},{9,25},{18,2},{26... | collective-permute-start | bytes 393224 | tf_op jit(solution)/shard_map/ppermute | solution.py:596
  26.8 5.9 %copy-start.1 = (bf16[16,512]{1,0:T(8,128)(2,1)S(1)}, bf16[16,512]{1,0:T(8,128)(2,1)}, u32[]{:S(2)}) copy-start(bf16[16,512]{1,0:T(8,128)(2,1)} %shard_map.121.embedded_hbm.embedded_ref) | copy-start | bytes 49156
  26.8 5.9 %copy-start.3 = (f32[1,256]{1,0:T(1,128)S(1)}, f32[1,256]{1,0:T(1,128)}, u32[]{:S(2)}) copy-start(f32[1,256]{1,0:T(1,128)} %gain_ref.1) | copy-start | bytes 3076
  31.0 1.7 %collective-permute-start.7 = (f32[328,256]{1,0:T(8,128)S(1)}, f32[328,256]{1,0:T(8,128)S(1)}, u32[]{:S(2)}, u32[]{:S(2)}) collective-permute-start(f32[328,256]{1,0:T(8,128)S(1)} %get-tuple-element.55), channel_id=1, source_target_pairs={{0,8},{8,0},{16,24},{24,16},{1,9},{9,1},{17,25},{25,17},{2,10},{10... | collective-permute-start | bytes 1007624 | tf_op jit(solution)/shard_map/ppermute | solution.py:662

commit v5 on v4

--- a/solution.py
+++ b/solution.py
@@ -308,7 +308,8 @@
     return copies
 
 
-def embed_kernel(times_ref, labels_ref, table_hbm, time_weight_hbm, embedded_ref, table_ref, time_weight_ref, sems):
+def embed_kernel(times_ref, labels_ref, table_hbm, time_weight_hbm, *refs):
+    embedded_ref, turned_ref, table_ref, time_weight_ref, sems = refs
     pairs = [(time_weight_hbm, time_weight_ref)]
     pairs += [(table_hbm.at[pl.ds(labels_ref[i] // 8, 1)], table_ref.at[pl.ds(i, 1)]) for i in range(PAIR)]
     copies = start_all(pairs, sems)
@@ -325,7 +326,9 @@
         copy.wait()
     timed = jnp.dot(sinusoid, time_weight_ref[...], preferred_element_type=jnp.float32)
     timed = timed + jnp.where(spot % 2 == 0, label_row(0), label_row(1))
-    embedded_ref[...] = (timed * sigmoid(timed)).astype(jnp.bfloat16)
+    embedded = timed * sigmoid(timed)
+    embedded_ref[...] = embedded.astype(jnp.bfloat16)
+    turned_ref[...] = embedded.T.astype(jnp.bfloat16)
 
 
 def modulate_kernel(embedded_hbm, mod_weight_hbm, bias_hbm, gain_hbm, keep_ref, send_ref, *scratch):
@@ -483,9 +486,9 @@
     for k in range(MOD_PARTS):
         place = slice(k * size, (k + 1) * size)
         mod_ref[place, :] = lax.dot_general(
-            embedded_ref[:, place],
+            embedded_ref[place, :],
             pieces,
-            (((0,), (0,)), ((), ())),
+            (((1,), (0,)), ((), ())),
             preferred_element_type=jnp.float32,
         )
         copies.append(pltpu.make_async_copy(mod_ref.at[place], mod_hbm.at[place], sems.at[k]))
@@ -547,10 +550,10 @@
     while True:
         far = lax.ppermute(near, "space", [(i, i ^ bit) for i in range(spaces)])
         if not waiting:
-            (embedded,) = call(
+            embedded, turned_embedded = call(
                 embed_kernel,
                 [SMEM, SMEM, ANY, ANY],
-                [shape((16, width), bf16)],
+                [shape((16, width), bf16), shape((width, 16), bf16)],
                 [
                     pltpu.VMEM((PAIR, 8, width), bf16),
                     pltpu.VMEM(time_weight.shape, bf16),
@@ -672,7 +675,7 @@
         out_specs=[ANY] * 3,
         scratch_shapes=[pltpu.VMEM(*final) for final in finals] + [pltpu.SemaphoreType.DMA((MOD_PARTS + 2,))],
         compiler_params=pltpu.CompilerParams(vmem_limit_bytes=CHAIN_LIMIT),
-    )(keep, other, embedded, norm_gain)
+    )(keep, other, turned_embedded, norm_gain)
     return (grads.reshape(1, images, row_count, cols, channels), conv_grad[None], mod_grad[None])
 
 

time: 34.4 us -> 34.6 us (level)
  no operation moved by 1% of the time
where the time goes in v5:
time: 34.6 us; the launch traced here: 34.1 us
  Pallas kernels  10.8 us (31%)
  waiting for transfers between devices  10.8 us (31%)
  starting transfers between devices  10.3 us (30%)
  other arithmetic  0.76 us (2%)
  between operations  0.76 us (2%)
  local copies, waits for them, and re-layouts  0.71 us (2%)
    ppermute x2, waiting for transfers between devices, hop(): return lax.ppermute(value, 'segment', pairs + [(b, a) for a, b in pairs])  7.22 us
    ppermute x3, starting transfers between devices, shards(): far = lax.ppermute(near, 'space', [(i, i ^ bit) for i in range(spaces)])  6.9 us
    ppermute x2, starting transfers between devices, hop(): return lax.ppermute(value, 'segment', pairs + [(b, a) for a, b in pairs])  2.78 us
    pallas_call x1, Pallas kernels, shards(): call(embed_kernel, [SMEM, SMEM, ANY, ANY], [shape((16, width), bf16), sha...  2.51 us
    pallas_call x1, Pallas kernels, shards(): call(modulate_kernel, [ANY] * 4, [shape((8, channels), f32)] * 2, [pltpu....  1.88 us
    pallas_call x1, Pallas kernels, shards(): call(functools.partial(backward_kernel, sh, active), [VMEM] * 10, [pack_s...  1.67 us
    ppermute x1, waiting for transfers between devices, shards(): other = lax.ppermute(send, 'segment', swap)  1.63 us
    pallas_call x1, Pallas kernels, shards(): call(functools.partial(forward_kernel, sh, 0, (order, far_order)), [VMEM]...  1.58 us
  transfers between devices with their start and end apart: 8, of which 6 were waited for; matrix products, arithmetic and copies ran while one was open for 2% of the time, Pallas kernels for 18%

profile of v5, /device:TPU:0, one launch (start us, length us, event | category | flops | bytes accessed | tf_op | source)
XLA Modules:
  0.0 34.1 jit_solution(2676796174167418600)
XLA Ops:
  0.6 0.5 %collective-permute-start.3 = (bf16[2304,256]{1,0:T(8,128)(2,1)}, bf16[2304,256]{1,0:T(8,128)(2,1)S(1)}, u32[]{:S(2)}, u32[]{:S(2)}) collective-permute-start(bf16[2304,256]{1,0:T(8,128)(2,1)} %bitcast.7), channel_id=1, source_target_pairs={{0,8},{8,0},{16,24},{24,16},{1,9},{9,1},{17,25},{25,17},{2,10},{10... | collective-permute-start | bytes 3538952 | tf_op jit(solution)/shard_map/ppermute | solution.py:542
  1.2 0.7 %dynamic-slice_select_fusion = bf16[1,2,16,256]{3,2,1,0:T(8,128)(2,1)S(1)} fusion(bf16[2,2,16,256]{3,2,1,0:T(8,128)(2,1)} %param.11, s32[]{:T(128)S(6)} %select_n.27, bf16[2,2,16,256]{3,2,1,0:T(8,128)(2,1)} %param.10, pred[]{:T(512)S(6)} %eq.5), kind=kLoop, calls=%fused_computation.2 | loop fusion | flops 8192 | bytes 49157 | tf_op jit(solution)/shard_map/jit(_where)/select_n | solution.py:543
  1.9 3.7 %collective-permute-start = (bf16[1,32,256]{2,1,0:T(8,128)(2,1)S(1)}, bf16[1,32,256]{2,1,0:T(8,128)(2,1)S(1)}, u32[]{:S(2)}, u32[]{:S(2)}) collective-permute-start(bf16[1,32,256]{2,1,0:T(8,128)(2,1)S(1)} %bitcast.11), channel_id=1, source_target_pairs={{0,4},{1,5},{2,6},{3,7},{4,0},{5,1},{6,2},{7,3},{8,12},{9,13},{10,... | collective-permute-start | bytes 49160 | tf_op jit(solution)/shard_map/ppermute | solution.py:551
  5.6 2.5 %shard_map.121 = (bf16[16,512]{1,0:T(8,128)(2,1)}, bf16[512,16]{1,0:T(8,128)(2,1)}) custom-call(s32[2]{0:T(128)} %times_ref.1, s32[2]{0:T(128)} %labels_ref.1, bf16[125,8,512]{2,1,0:T(8,128)(2,1)} %bitcast.9, bf16[128,512]{1,0:T(8,128)(2,1)} %time_weight_hbm.1), custom_call_target="tpu_custom_call" | custom-call | flops 1048576 | bytes 4194304 | tf_op jit(solution)/shard_map/pallas_call | solution.py:553
  8.1 1.6 %collective-permute-start.1 = (bf16[2,32,256]{2,1,0:T(8,128)(2,1)S(1)}, bf16[2,32,256]{2,1,0:T(8,128)(2,1)S(1)}, u32[]{:S(2)}, u32[]{:S(2)}) collective-permute-start(bf16[2,32,256]{2,1,0:T(8,128)(2,1)S(1)} %pad_maximum_fusion.1), channel_id=1, source_target_pairs={{0,2},{1,3},{2,0},{3,1},{4,6},{5,7},{6,4},{7,5},{8,10},{9,11},{10,... | collective-permute-start | bytes 98312 | tf_op jit(solution)/shard_map/ppermute | solution.py:551
  9.8 1.9 %shard_map.122 = (f32[8,256]{1,0:T(8,128)}, f32[8,256]{1,0:T(8,128)}) custom-call(bf16[16,512]{1,0:T(8,128)(2,1)} %get-tuple-element.35.embedded_hbm, bf16[512,512]{1,0:T(8,128)(2,1)} %bitcast.10, f32[1,512]{1,0:T(1,128)} %bias_hbm.1, f32[1,256]{1,0:T(1,128)} %gain_ref.1), custom_call_target="tpu_custom_call" | custom-call | flops 1048576 | bytes 4194304 | tf_op jit(solution)/shard_map/pallas_call | solution.py:569
  11.7 0.4 %collective-permute-done.1 = bf16[2,32,256]{2,1,0:T(8,128)(2,1)S(1)} collective-permute-done((bf16[2,32,256]{2,1,0:T(8,128)(2,1)S(1)}, bf16[2,32,256]{2,1,0:T(8,128)(2,1)S(1)}, u32[]{:S(2)}, u32[]{:S(2)}) %collective-permute-start.1) | collective-permute-done | bytes 32800 | tf_op jit(solution)/shard_map/ppermute | solution.py:551
  12.1 1.6 %collective-permute-start.2 = (bf16[4,32,256]{2,1,0:T(8,128)(2,1)S(1)}, bf16[4,32,256]{2,1,0:T(8,128)(2,1)S(1)}, u32[]{:S(2)}, u32[]{:S(2)}) collective-permute-start(bf16[4,32,256]{2,1,0:T(8,128)(2,1)S(1)} %pad_maximum_fusion.refs_0_), channel_id=1, source_target_pairs={{0,1},{1,0},{2,3},{3,2},{4,5},{5,4},{6,7},{7,6},{8,9},{9,8},{10,11... | collective-permute-start | bytes 196616 | tf_op jit(solution)/shard_map/ppermute | solution.py:551
  13.7 1.4 %collective-permute-done.4.mod_other_any = f32[8,256]{1,0:T(8,128)S(1)} collective-permute-done((f32[8,256]{1,0:T(8,128)}, f32[8,256]{1,0:T(8,128)S(1)}, u32[]{:S(2)}, u32[]{:S(2)}) %collective-permute-start.4) | collective-permute-done | bytes 8224 | tf_op jit(solution)/shard_map/ppermute | solution.py:584
  15.1 0.7 %copy-done.2 = f32[8,256]{1,0:T(8,128)S(1)} copy-done((f32[8,256]{1,0:T(8,128)S(1)}, f32[8,256]{1,0:T(8,128)}, u32[]{:S(2)}) %copy-start.2) | copy-done | bytes 8216
  15.8 0.5 %shard_map.123 = (bf16[2,2304,256]{2,1,0:T(8,128)(2,1)S(1)}, f32[8,256]{1,0:T(8,128)S(1)}) custom-call(bf16[2304,256]{1,0:T(8,128)(2,1)S(1)} %bitcast.8, bf16[2304,256]{1,0:T(8,128)(2,1)S(1)} %collective-permute-done.3.other_any, f32[8,256]{1,0:T(8,128)S(1)} %copy-done.2, f32[8,256]{1,0:T(8,128)S(1)} %collective-permute-done.4.mod_other_any), custom_call_target="tpu_custom_call" | custom-call | flops 1048576 | bytes 4194304 | tf_op jit(solution)/shard_map/pallas_call | solution.py:585
  16.3 0.2 collective-permute-done.2.refs_1_
  16.5 1.6 %shard_map.124 = (bf16[256,256]{1,0:T(8,128)(2,1)S(1)}, bf16[256,256]{1,0:T(8,128)(2,1)S(1)}, bf16[256,256]{1,0:T(8,128)(2,1)S(1)}) custom-call(bf16[4,32,256]{2,1,0:T(8,128)(2,1)S(1)} %pad_maximum_fusion.refs_0_, bf16[4,32,256]{2,1,0:T(8,128)(2,1)S(1)} %collective-permute-done.2.refs_1_, f32[8,256]{1,0:T(8,128)S(1)} %get-tuple-element.41.refs_2_.params_ref.refs_3_, ...), custom_call_target="tpu_custom_call" | custom-call | tf_op jit(solution)/shard_map/pallas_call | solution.py:601
  18.1 0.1 collective-permute-start.5
  18.1 0.7 %shard_map.125 = (bf16[3,288,256]{2,1,0:T(8,128)(2,1)S(1)}, bf16[2,2304,256]{2,1,0:T(8,128)(2,1)S(1)}) custom-call(bf16[256,256]{1,0:T(8,128)(2,1)S(1)} %get-tuple-element.43.up_ref.x_ref.refs_0_, bf16[2,2304,256]{2,1,0:T(8,128)(2,1)S(1)} %get-tuple-element.42.refs_3_.weights_ref.weights), custom_call_target="tpu_custom_call" | custom-call | flops 1048576 | bytes 4194304 | tf_op jit(solution)/shard_map/pallas_call | solution.py:635
  18.8 4.7 %collective-permute-done.5.x_ref = bf16[256,256]{1,0:T(8,128)(2,1)S(1)} collective-permute-done((bf16[256,256]{1,0:T(8,128)(2,1)S(1)}, bf16[256,256]{1,0:T(8,128)(2,1)S(1)}, u32[]{:S(2)}, u32[]{:S(2)}) %collective-permute-start.5) | collective-permute-done | bytes 131104 | tf_op jit(solution)/shard_map/ppermute | solution.py:599
  23.6 2.7 %collective-permute-start.6 = (bf16[256,256]{1,0:T(8,128)(2,1)S(1)}, bf16[256,256]{1,0:T(8,128)(2,1)S(1)}, u32[]{:S(2)}, u32[]{:S(2)}) collective-permute-start(bf16[256,256]{1,0:T(8,128)(2,1)S(1)} %get-tuple-element.48.grad_ref), channel_id=1, source_target_pairs={{16,0},{24,8},{0,16},{8,24},{17,1},{25,9},{1,17},{9,25},{18,2},{26... | collective-permute-start | bytes 393224 | tf_op jit(solution)/shard_map/ppermute | solution.py:599
  26.3 0.6 %shard_map.127 = (bf16[2,256,256]{2,1,0:T(8,128)(2,1)S(1)}, f32[2,256,256]{2,1,0:T(8,128)S(1)}, f32[2,8,256]{2,1,0:T(8,128)S(1)}) custom-call(bf16[256,256]{1,0:T(8,128)(2,1)S(1)} %get-tuple-element.43.up_ref.x_ref.refs_0_, bf16[256,256]{1,0:T(8,128)(2,1)S(1)} %get-tuple-element.44.middle_ref.refs_1_, f32[8,256]{1,0:T(8,128)S(1)} %get-tuple-element.41.refs_2_.params_ref.refs_3_), custom_call_target="tpu_custom_call" | custom-call | flops 1048576 | bytes 4194304 | tf_op jit(solution)/shard_map/pallas_call | solution.py:620
  26.9 0.0 copy-start.1
  27.0 2.5 %collective-permute-done.6.refs_2_ = bf16[256,256]{1,0:T(8,128)(2,1)S(1)} collective-permute-done((bf16[256,256]{1,0:T(8,128)(2,1)S(1)}, bf16[256,256]{1,0:T(8,128)(2,1)S(1)}, u32[]{:S(2)}, u32[]{:S(2)}) %collective-permute-start.6) | collective-permute-done | bytes 131104 | tf_op jit(solution)/shard_map/ppermute | solution.py:599
  29.4 1.7 %shard_map.129 = (f32[328,256]{1,0:T(8,128)S(1)}, f32[328,256]{1,0:T(8,128)S(1)}) custom-call(bf16[256,256]{1,0:T(8,128)(2,1)S(1)} %get-tuple-element.43.up_ref.x_ref.refs_0_, bf16[256,256]{1,0:T(8,128)(2,1)S(1)} %get-tuple-element.44.middle_ref.refs_1_, ...), custom_call_target="tpu_custom_call", output_to_operand_aliasing={{0}: (8, {}), {1}: (9, {})} | custom-call | tf_op jit(solution)/shard_map/pallas_call | solution.py:658
  31.1 0.1 collective-permute-start.7
  31.2 1.6 %collective-permute-done.7.other_ref = f32[328,256]{1,0:T(8,128)S(1)} collective-permute-done((f32[328,256]{1,0:T(8,128)S(1)}, f32[328,256]{1,0:T(8,128)S(1)}, u32[]{:S(2)}, u32[]{:S(2)}) %collective-permute-start.7) | collective-permute-done | bytes 335904 | tf_op jit(solution)/shard_map/ppermute | solution.py:665
  32.8 1.3 %shard_map.130 = (bf16[2,32,256]{2,1,0:T(8,128)(2,1)}, f32[288,256]{1,0:T(8,128)}, f32[512,512]{1,0:T(8,128)}) custom-call(f32[328,256]{1,0:T(8,128)S(1)} %get-tuple-element.57.keep_ref, f32[328,256]{1,0:T(8,128)S(1)} %collective-permute-done.7.other_ref, bf16[512,16]{1,0:T(8,128)(2,1)S(1)} %copy-done.1, f32[1,256]{1,0:T(1,128)S(1)} %copy-done.3), custom_call_target="tpu_custom_call" | custom-call | tf_op jit(solution)/shard_map/pallas_call | solution.py:671
  (13 shorter events, 0.1 us)
Async XLA Ops:
  0.6 14.5 %copy-start = (bf16[1,3,3,256,256]{4,3,2,1,0:T(8,128)(2,1)S(1)}, bf16[1,3,3,256,256]{4,3,2,1,0:T(8,128)(2,1)}, u32[]{:S(2)}) copy-start(bf16[1,3,3,256,256]{4,3,2,1,0:T(8,128)(2,1)} %param.16) | copy-start | bytes 3538948
  0.6 14.4 %collective-permute-start.3 = (bf16[2304,256]{1,0:T(8,128)(2,1)}, bf16[2304,256]{1,0:T(8,128)(2,1)S(1)}, u32[]{:S(2)}, u32[]{:S(2)}) collective-permute-start(bf16[2304,256]{1,0:T(8,128)(2,1)} %bitcast.7), channel_id=1, source_target_pairs={{0,8},{8,0},{16,24},{24,16},{1,9},{9,1},{17,25},{25,17},{2,10},{10... | collective-permute-start | bytes 3538952 | tf_op jit(solution)/shard_map/ppermute | solution.py:542
  1.9 6.2 %collective-permute-start = (bf16[1,32,256]{2,1,0:T(8,128)(2,1)S(1)}, bf16[1,32,256]{2,1,0:T(8,128)(2,1)S(1)}, u32[]{:S(2)}, u32[]{:S(2)}) collective-permute-start(bf16[1,32,256]{2,1,0:T(8,128)(2,1)S(1)} %bitcast.11), channel_id=1, source_target_pairs={{0,4},{1,5},{2,6},{3,7},{4,0},{5,1},{6,2},{7,3},{8,12},{9,13},{10,... | collective-permute-start | bytes 49160 | tf_op jit(solution)/shard_map/ppermute | solution.py:551
  8.1 4.0 %collective-permute-start.1 = (bf16[2,32,256]{2,1,0:T(8,128)(2,1)S(1)}, bf16[2,32,256]{2,1,0:T(8,128)(2,1)S(1)}, u32[]{:S(2)}, u32[]{:S(2)}) collective-permute-start(bf16[2,32,256]{2,1,0:T(8,128)(2,1)S(1)} %pad_maximum_fusion.1), channel_id=1, source_target_pairs={{0,2},{1,3},{2,0},{3,1},{4,6},{5,7},{6,4},{7,5},{8,10},{9,11},{10,... | collective-permute-start | bytes 98312 | tf_op jit(solution)/shard_map/ppermute | solution.py:551
  12.1 4.3 %collective-permute-start.2 = (bf16[4,32,256]{2,1,0:T(8,128)(2,1)S(1)}, bf16[4,32,256]{2,1,0:T(8,128)(2,1)S(1)}, u32[]{:S(2)}, u32[]{:S(2)}) collective-permute-start(bf16[4,32,256]{2,1,0:T(8,128)(2,1)S(1)} %pad_maximum_fusion.refs_0_), channel_id=1, source_target_pairs={{0,1},{1,0},{2,3},{3,2},{4,5},{5,4},{6,7},{7,6},{8,9},{9,8},{10,11... | collective-permute-start | bytes 196616 | tf_op jit(solution)/shard_map/ppermute | solution.py:551
  13.7 1.4 %collective-permute-start.4 = (f32[8,256]{1,0:T(8,128)}, f32[8,256]{1,0:T(8,128)S(1)}, u32[]{:S(2)}, u32[]{:S(2)}) collective-permute-start(f32[8,256]{1,0:T(8,128)} %get-tuple-element.40), channel_id=1, source_target_pairs={{0,8},{8,0},{16,24},{24,16},{1,9},{9,1},{17,25},{25,17},{2,10},{10... | collective-permute-start | bytes 24584 | tf_op jit(solution)/shard_map/ppermute | solution.py:584
  15.1 0.7 %copy-start.2 = (f32[8,256]{1,0:T(8,128)S(1)}, f32[8,256]{1,0:T(8,128)}, u32[]{:S(2)}) copy-start(f32[8,256]{1,0:T(8,128)} %get-tuple-element.39.mod_keep_any) | copy-start | bytes 24580
  18.1 5.5 %collective-permute-start.5 = (bf16[256,256]{1,0:T(8,128)(2,1)S(1)}, bf16[256,256]{1,0:T(8,128)(2,1)S(1)}, u32[]{:S(2)}, u32[]{:S(2)}) collective-permute-start(bf16[256,256]{1,0:T(8,128)(2,1)S(1)} %get-tuple-element.45), channel_id=1, source_target_pairs={{0,16},{8,24},{16,0},{24,8},{1,17},{9,25},{17,1},{25,9},{2,18},{10... | collective-permute-start | bytes 393224 | tf_op jit(solution)/shard_map/ppermute | solution.py:599
  23.6 5.9 %collective-permute-start.6 = (bf16[256,256]{1,0:T(8,128)(2,1)S(1)}, bf16[256,256]{1,0:T(8,128)(2,1)S(1)}, u32[]{:S(2)}, u32[]{:S(2)}) collective-permute-start(bf16[256,256]{1,0:T(8,128)(2,1)S(1)} %get-tuple-element.48.grad_ref), channel_id=1, source_target_pairs={{16,0},{24,8},{0,16},{8,24},{17,1},{25,9},{1,17},{9,25},{18,2},{26... | collective-permute-start | bytes 393224 | tf_op jit(solution)/shard_map/ppermute | solution.py:599
  26.9 5.9 %copy-start.1 = (bf16[512,16]{1,0:T(8,128)(2,1)S(1)}, bf16[512,16]{1,0:T(8,128)(2,1)}, u32[]{:S(2)}) copy-start(bf16[512,16]{1,0:T(8,128)(2,1)} %get-tuple-element.59.embedded_ref) | copy-start | bytes 49156
  26.9 5.9 %copy-start.3 = (f32[1,256]{1,0:T(1,128)S(1)}, f32[1,256]{1,0:T(1,128)}, u32[]{:S(2)}) copy-start(f32[1,256]{1,0:T(1,128)} %gain_ref.1) | copy-start | bytes 3076
  31.1 1.7 %collective-permute-start.7 = (f32[328,256]{1,0:T(8,128)S(1)}, f32[328,256]{1,0:T(8,128)S(1)}, u32[]{:S(2)}, u32[]{:S(2)}) collective-permute-start(f32[328,256]{1,0:T(8,128)S(1)} %get-tuple-element.58), channel_id=1, source_target_pairs={{0,8},{8,0},{16,24},{24,16},{1,9},{9,1},{17,25},{25,17},{2,10},{10... | collective-permute-start | bytes 1007624 | tf_op jit(solution)/shard_map/ppermute | solution.py:665
